TPU v7x, 512 devices: a whole 4x4x16 slice. The times are simulated.
512 devices in a mesh: group: 8 (over z_lo), member: 64 (over x, z_hi, y, core).
Axes of the slice: x: 4, y: 4, z: 16 (z_hi: 2, z_lo: 8; z = z_hi * 8 + z_lo), core: 2. Of those that a mesh axis runs over, the one named last changes fastest.
Arguments:
- replay_embed: bfloat16 [16384, 24, 1024], P(('group', 'member')), may hold values from -6 to 6
- replay_steps: bfloat16 [16384, 2, 24], P(('group', 'member')), as said below
- replay_actions: int32 [16384, 24], P(('group', 'member')), may hold values from 0 to 17
- replay_lengths: int32 [16384], P(('group', 'member')), may hold values from 1 to 24, as said below
- sample_owner: int32 [16384, 1], P(('group', 'member')), may hold values from 0 to 63; in each aligned block of 32 rows (0 to 31, 32 to 63, ...) no two rows name the same one
- sample_slot: int32 [16384], P(('group', 'member')), may hold values from 0 to 31
- sample_weight: float32 [16384], P(('group', 'member')), may hold values from 0.1 to 1
- norm_gain: float32 [1024], replicated
- w_query: bfloat16 [1024, 512], P('member')
- w_key: bfloat16 [1024, 512], P('member')
- w_value: bfloat16 [1024, 512], P('member'), may hold values from -0.1875 to 0.1875
- w_out: bfloat16 [512, 1024], P('member'), may hold values from -0.25 to 0.25
- q_head: bfloat16 [1024, 18], replicated, may hold values from -0.1875 to 0.1875
- policy_head: bfloat16 [1024, 18], replicated
Outputs:
- grad_value: float32 [1024, 512], P('member')
- grad_out: float32 [512, 1024], P('member')
Inputs may be any that keep to these rules, and one draw needn't show every extreme that they name: `sample_owner`: the member of the row's own learner group that holds the sampled sequence; among the 32 rows of one device no member is named more than 1 times. `replay_lengths`: steps from a sequence's length on are padding. `replay_steps`: row 0 holds rewards, row 1 the behaviour policy's probability of the taken action, positive and at most 1.
All inputs are finite; a program needn't handle non-finite values.
Results may differ from a plain program's by a relative error of at most 0.0073.
Values may be sent and summed in bfloat16 or wider, within the bound.
No kernel may reach another device: no remote copies, remote signals or barrier semaphores. Data moves between devices by JAX's collectives and lax.ppermute only.
A program may use at most 64 MiB of HBM per device.

v0:
```python
import jax
import jax.numpy as jnp
from jax import lax
from jax.sharding import PartitionSpec as P

HEAD_DIM = 128


trace_lambda = 0.95
discount = 0.997
clip_norm = 1024.0


def normalize_rows(embeds, gain_row):
    values = embeds.astype(jnp.float32)
    meansq = jnp.mean(values * values, axis=-1, keepdims=True)
    return (values * lax.rsqrt(meansq + 1e-06) * gain_row).astype(jnp.bfloat16)


def retrace_grad(q_values, policy, actions, step_data, lengths, weights):
    num_seq, seq_len, action_count = q_values.shape
    picker = (actions[..., None] == jnp.arange(action_count)[None, None, :]).astype(jnp.float32)
    rewards = step_data[:, 0, :].astype(jnp.float32)
    behaviour = step_data[:, 1, :].astype(jnp.float32)
    values = jnp.sum(policy * q_values, axis=-1)
    taken_q = jnp.sum(picker * q_values, axis=-1)
    traces = trace_lambda * jnp.minimum(1.0, jnp.sum(picker * policy, axis=-1) / behaviour)
    positions = jnp.arange(seq_len)
    live_mask = (positions[None, :] < lengths[:, None]).astype(jnp.float32)
    onward = (positions[None, :] + 1 < lengths[:, None]).astype(jnp.float32)
    padding = jnp.zeros((num_seq, 1), jnp.float32)
    next_values = jnp.concatenate([values[:, 1:], padding], axis=1)
    next_traces = jnp.concatenate([traces[:, 1:], padding], axis=1)
    next_taken = jnp.concatenate([taken_q[:, 1:], padding], axis=1)

    def stepper(later_target, inputs):
        reward_now, continues, value_next, trace_next, taken_next = inputs
        target_now = reward_now + discount * continues * (
            value_next + trace_next * (later_target - taken_next)
        )
        return (target_now, target_now)

    last_target, targets = lax.scan(
        stepper,
        jnp.zeros((num_seq,), jnp.float32),
        (rewards.T, onward.T, next_values.T, next_traces.T, next_taken.T),
        reverse=True,
    )
    errors = weights[:, None] * live_mask * (taken_q - targets.T)
    return errors[..., None] * picker


def sequence_grads(
    embeds,
    step_data,
    actions,
    lengths,
    weights,
    gain_row,
    w_query,
    w_key,
    w_value,
    w_out,
    q_head,
    policy_head,
):
    num_seq, seq_len, features = embeds.shape
    normed = normalize_rows(embeds, gain_row).reshape(num_seq * seq_len, features)

    def project(matrix):
        return (
            jnp.dot(normed, matrix, preferred_element_type=jnp.float32)
            .astype(jnp.bfloat16)
            .reshape(num_seq, seq_len, -1, HEAD_DIM)
        )

    queries = project(w_query)
    keys_all = project(w_key)
    values_all = project(w_value)
    scores = jnp.einsum(
        "bqhe,bkhe->bhqk", queries, keys_all, preferred_element_type=jnp.float32
    ) * HEAD_DIM ** (-0.5)
    positions = jnp.arange(seq_len)
    causal = positions[None, :] <= positions[:, None]
    allowed = causal[None, None, :, :] & (
        positions[None, None, None, :] < lengths[:, None, None, None]
    )
    scores = jnp.where(allowed, scores, -1e30)
    row_peak = jnp.max(scores, axis=-1, keepdims=True)
    weights_exp = jnp.where(allowed, jnp.exp(scores - row_peak), 0.0)
    attn_probs = (weights_exp / jnp.sum(weights_exp, axis=-1, keepdims=True)).astype(jnp.bfloat16)
    mixed_heads = jnp.einsum(
        "bhqk,bkhe->bqhe", attn_probs, values_all, preferred_element_type=jnp.float32
    )
    mixed_heads = mixed_heads.astype(jnp.bfloat16).reshape(num_seq * seq_len, -1)
    hidden = embeds.reshape(num_seq * seq_len, features).astype(jnp.float32) + jnp.dot(
        mixed_heads, w_out, preferred_element_type=jnp.float32
    )
    hidden = hidden.astype(jnp.bfloat16)
    q_values = jnp.dot(hidden, q_head, preferred_element_type=jnp.float32)
    policy = jax.nn.softmax(
        jnp.dot(hidden, policy_head, preferred_element_type=jnp.float32), axis=-1
    )
    d_qvalues = retrace_grad(
        q_values.reshape(num_seq, seq_len, -1),
        policy.reshape(num_seq, seq_len, -1),
        actions,
        step_data,
        lengths,
        weights,
    ).reshape(num_seq * seq_len, -1)
    d_hidden = jnp.dot(
        d_qvalues, q_head.astype(jnp.float32).T, precision=lax.Precision.HIGHEST
    ).astype(jnp.bfloat16)
    grad_out = lax.dot_general(
        mixed_heads, d_hidden, (((0,), (0,)), ((), ())), preferred_element_type=jnp.float32
    )
    d_mixed = lax.dot_general(
        d_hidden, w_out, (((1,), (1,)), ((), ())), preferred_element_type=jnp.float32
    )
    d_mixed = d_mixed.astype(jnp.bfloat16).reshape(num_seq, seq_len, -1, HEAD_DIM)
    d_value = jnp.einsum("bhqk,bqhe->bkhe", attn_probs, d_mixed, preferred_element_type=jnp.float32)
    d_value = d_value.astype(jnp.bfloat16).reshape(num_seq * seq_len, -1)
    grad_value = lax.dot_general(
        normed, d_value, (((0,), (0,)), ((), ())), preferred_element_type=jnp.float32
    )
    return (grad_value, grad_out)


def per_device(
    replay_embed,
    replay_steps,
    replay_actions,
    replay_lengths,
    sample_owner,
    sample_slot,
    sample_weight,
    norm_gain,
    w_query,
    w_key,
    w_value,
    w_out,
    q_head,
    policy_head,
):
    members = lax.axis_size("member")
    full_query, full_key, full_value, full_out = (
        lax.all_gather(w_query, "member", axis=0, tiled=True),
        lax.all_gather(w_key, "member", axis=0, tiled=True),
        lax.all_gather(w_value, "member", axis=0, tiled=True),
        lax.all_gather(w_out, "member", axis=0, tiled=True),
    )
    owners = sample_owner[:, 0]
    row_count = owners.shape[0]
    seq_steps = replay_embed.shape[1]
    capacity = max(1, 2 * row_count // members)
    positions = jnp.arange(row_count)
    earlier = (owners[:, None] == owners[None, :]) & (positions[None, :] < positions[:, None])
    places = owners * capacity + jnp.sum(earlier, axis=1)
    matches = places[:, None] == jnp.arange(members * capacity)[None, :]
    wanted = jnp.sum(jnp.where(matches, sample_slot[:, None], 0), axis=0).reshape(members, capacity)
    incoming = lax.all_to_all(wanted, "member", split_axis=0, concat_axis=0, tiled=True).reshape(-1)
    sent_embed = jnp.take(replay_embed, incoming, axis=0).reshape(members, capacity, seq_steps, -1)
    sent_steps = jnp.take(replay_steps, incoming, axis=0).reshape(members, capacity, 2, seq_steps)
    got_embed, got_steps = (
        lax.all_to_all(sent_embed, "member", split_axis=0, concat_axis=0, tiled=True),
        lax.all_to_all(sent_steps, "member", split_axis=0, concat_axis=0, tiled=True),
    )
    sent_actions = jnp.take(replay_actions, incoming, axis=0).reshape(members, capacity, seq_steps)
    sent_lengths = jnp.take(replay_lengths, incoming, axis=0).reshape(members, capacity)
    got_actions, got_lengths = (
        lax.all_to_all(sent_actions, "member", split_axis=0, concat_axis=0, tiled=True),
        lax.all_to_all(sent_lengths, "member", split_axis=0, concat_axis=0, tiled=True),
    )
    embeds = jnp.take(got_embed.reshape(members * capacity, seq_steps, -1), places, axis=0)
    step_data = jnp.take(got_steps.reshape(members * capacity, 2, seq_steps), places, axis=0)
    actions = jnp.take(got_actions.reshape(members * capacity, seq_steps), places, axis=0)
    lengths = jnp.take(got_lengths.reshape(members * capacity), places, axis=0)
    grad_value, grad_out = sequence_grads(
        embeds,
        step_data,
        actions,
        lengths,
        sample_weight,
        norm_gain,
        full_query,
        full_key,
        full_value,
        full_out,
        q_head,
        policy_head,
    )
    shard_value, shard_out = (
        lax.psum_scatter(grad_value, "member", scatter_dimension=0, tiled=True),
        lax.psum_scatter(grad_out, "member", scatter_dimension=0, tiled=True),
    )
    shard_value, shard_out = lax.psum((shard_value, shard_out), "group")
    local_squares = jnp.sum(shard_value * shard_value) + jnp.sum(shard_out * shard_out)
    squares = lax.psum(local_squares, "member")
    clip_scale = jnp.minimum(1.0, clip_norm / jnp.sqrt(squares))
    return (shard_value * clip_scale, shard_out * clip_scale)


def solution(mesh):
    return jax.shard_map(
        per_device,
        mesh=mesh,
        in_specs=(
            P(("group", "member"), None, None),
            P(("group", "member"), None, None),
            P(("group", "member"), None),
            P(("group", "member")),
            P(("group", "member"), None),
            P(("group", "member")),
            P(("group", "member")),
            P(),
            P("member", None),
            P("member", None),
            P("member", None),
            P("member", None),
            P(),
            P(),
        ),
        out_specs=(P("member", None), P("member", None)),
        check_vma=False,
    )
```

profile of v0, /device:TPU:1, one launch (start us, length us, event | category | flops | bytes accessed | tf_op | source)
XLA Modules:
  0.0 2158.5 jit_solution(10841592636539081855)
XLA Ops:
  7.2 1.0 convert_reduce_fusion
  8.1 0.7 fusion.46
  8.8 0.7 select_reduce_fusion.2
  9.6 0.7 copy.78
  10.3 22.2 %all-to-all-start = ((s32[64,1,1]{2,1,0:T(1,128)}), s32[64,1,1]{2,1,0:T(1,128)S(1)}, u32[]{:S(2)}, u32[]{:S(2)}) async-start(s32[64,1,1]{2,1,0:T(1,128)} %copy.78), calls=%async_computation | async-start | bytes 65536 | tf_op jit(solution)/shard_map/all_to_all | solution.py:162
  32.5 0.8 copy.79
  33.3 0.8 copy.90
  34.1 14.8 all-to-all-done
  48.9 1.2 reduce.3
  50.2 0.6 gather_fusion.2
  50.8 1.4 gather_fusion.4
  52.3 0.7 copy.84
  53.0 4.7 all-to-all-start.3
  57.7 0.7 bitcast_select_fusion.2
  58.4 0.6 gather_fusion.6
  59.1 15.2 all-to-all-done.3
  74.3 4.7 all-to-all-start.2
  79.0 0.8 fusion.39
  79.7 2.4 gather_fusion
  82.2 13.3 all-to-all-done.2
  95.5 4.7 all-to-all-start.4
  100.2 3.9 bitcast_select_fusion
  104.1 12.6 all-to-all-done.4
  116.7 5.6 all-to-all-start.1
  122.4 0.7 all-gather.5.cloned.1.call-update
  123.1 0.7 all-gather.9.cloned.1.call-update
  123.9 0.7 all-gather.7.cloned.1.call-update
  125.4 1.2 reduce.5
  126.6 0.7 gather_fusion.5
  128.4 0.6 gather_fusion.7
  129.2 82.5 %all-to-all-done.1 = bf16[64,1,24,1024]{3,2,1,0:T(8,128)(2,1)} async-done(((bf16[64,1,24,1024]{3,2,1,0:T(8,128)(2,1)}), bf16[64,1,24,1024]{3,2,1,0:T(8,128)(2,1)}, u32[]{:S(2)}, u32[]{:S(2)}) %all-to-all-start.1) | async-done | bytes 3145760 | tf_op jit(solution)/shard_map/all_to_all | solution.py:166
  211.7 2.5 gather_fusion.1
  214.8 1.5 bitcast_select_fusion.1
  216.4 99.9 %all-gather.5.cloned.1.call-done = bf16[1024,512]{1,0:T(8,128)(2,1)} async-done(((bf16[16,512]{1,0:T(8,128)(2,1)}), bf16[1024,512]{1,0:T(8,128)(2,1)}) %all-gather.5.cloned.1.call-update) | async-done | bytes 1048592 | tf_op jit(solution)/shard_map/all_gather | solution.py:150
  316.3 3.6 convolution_convert_fusion.6
  319.9 2.4 reshape.318
  322.3 90.9 %all-gather.9.cloned.1.call-done = bf16[1024,512]{1,0:T(8,128)(2,1)} async-done(((bf16[16,512]{1,0:T(8,128)(2,1)}), bf16[1024,512]{1,0:T(8,128)(2,1)}) %all-gather.9.cloned.1.call-update) | async-done | bytes 1048592 | tf_op jit(solution)/shard_map/all_gather | solution.py:149
  413.3 3.6 convolution_convert_fusion.4
  416.9 2.4 reshape.320
  419.3 90.9 %all-gather.7.cloned.1.call-done = bf16[1024,512]{1,0:T(8,128)(2,1)} async-done(((bf16[16,512]{1,0:T(8,128)(2,1)}), bf16[1024,512]{1,0:T(8,128)(2,1)}) %all-gather.7.cloned.1.call-update) | async-done | bytes 1048592 | tf_op jit(solution)/shard_map/all_gather | solution.py:148
  510.3 3.7 convolution_convert_fusion.5
  513.9 2.4 reshape.319
  516.4 3.6 fusion.52
  520.0 2.3 fusion.19
  522.2 1.2 copy.89
  523.4 1.7 fusion.14
  525.1 82.0 %all-gather.11.cloned.1.call-done = bf16[512,1024]{1,0:T(8,128)(2,1)} async-done(((bf16[8,1024]{1,0:T(8,128)(2,1)}), bf16[512,1024]{1,0:T(8,128)(2,1)}) %all-gather.11.cloned.1.call-update) | async-done | bytes 1048592 | tf_op jit(solution)/shard_map/all_gather | solution.py:151
  607.1 2.9 fusion.17
  612.2 1.9 while.17
  614.3 1.4 convolution_convert_fusion
  615.7 3.2 convolution_convert_fusion.2
  618.9 2.4 reshape.323
  621.4 2.2 fusion.20
  623.9 1.1 copy-done.1
  625.0 2.4 fusion.21
  627.4 3.4 fusion.24
  630.9 545.5 %reduce-scatter.3.cloned.1.call-done = f32[16,512]{1,0:T(8,128)} async-done(((f32[1024,512]{1,0:T(8,128)}), f32[16,512]{1,0:T(8,128)}) %reduce-scatter.3.cloned.1.call-update) | async-done | bytes 32784 | tf_op jit(solution)/shard_map/reduce_scatter | solution.py:194
  1176.5 564.6 %reduce-scatter.5.cloned.1.call-done = f32[8,1024]{1,0:T(8,128)} async-done(((f32[512,1024]{1,0:T(8,128)}), f32[8,1024]{1,0:T(8,128)}) %reduce-scatter.5.cloned.1.call-update) | async-done | bytes 32784 | tf_op jit(solution)/shard_map/reduce_scatter | solution.py:195
  1741.1 119.2 %all-reduce.6.cloned.1.call-done = (f32[16,512]{1,0:T(8,128)}, f32[8,1024]{1,0:T(8,128)}) async-done(((f32[16,512]{1,0:T(8,128)}, f32[8,1024]{1,0:T(8,128)}), (f32[16,512]{1,0:T(8,128)}, f32[8,1024]{1,0:T(8,128)})) %all-reduce.6.cloned.1.call-update) | async-done | bytes 65552 | tf_op jit(solution)/shard_map/psum | solution.py:197
  1860.3 1.4 multiply_reduce_fusion.2
  1861.6 1.4 multiply_reduce_fusion.1
  1864.3 283.9 %psum.23 = f32[]{:T(128)} all-reduce(f32[]{:T(128)S(6)} %add.157), channel_id=1, replica_groups=mesh['group'=8,'member'=64] {'member'}, use_global_device_ids=true, to_apply=%region_18.19 | all-reduce | flops 1 | bytes 8 | tf_op jit(solution)/shard_map/psum | solution.py:199
  2148.9 1.4 broadcast_multiply_fusion.1
  2150.2 1.4 broadcast_multiply_fusion
  (118 shorter events, 7.1 us)
Async XLA Ops:
  7.2 72.5 %copy-start = (bf16[32,24,1024]{2,1,0:T(8,128)(2,1)S(1)}, bf16[32,24,1024]{2,1,0:T(8,128)(2,1)}, u32[]{:S(2)}) copy-start(bf16[32,24,1024]{2,1,0:T(8,128)(2,1)} %param.16) | copy-start | bytes 4718596
  10.3 38.7 %all-to-all-start = ((s32[64,1,1]{2,1,0:T(1,128)}), s32[64,1,1]{2,1,0:T(1,128)S(1)}, u32[]{:S(2)}, u32[]{:S(2)}) async-start(s32[64,1,1]{2,1,0:T(1,128)} %copy.78), calls=%async_computation | async-start | bytes 65536 | tf_op jit(solution)/shard_map/all_to_all | solution.py:162
  53.0 21.2 all-to-all-start.3
  74.3 21.2 all-to-all-start.2
  95.5 21.2 all-to-all-start.4
  104.1 21.1 copy-start.6
  116.7 95.0 %all-to-all-start.1 = ((bf16[64,1,24,1024]{3,2,1,0:T(8,128)(2,1)}), bf16[64,1,24,1024]{3,2,1,0:T(8,128)(2,1)}, u32[]{:S(2)}, u32[]{:S(2)}) async-start(bf16[64,1,24,1024]{3,2,1,0:T(8,128)(2,1)} %bitcast_select_fusion), calls=%async_computation.1 | async-start | bytes 6291456 | tf_op jit(solution)/shard_map/all_to_all | solution.py:166
  122.3 193.9 %all-gather.5.cloned.1.call-start = ((), (), s32[]{:S(2)}) async-start(), calls=%async_computation.7 | async-start | bytes 1064960 | tf_op jit(solution)/shard_map/all_gather | solution.py:150
  123.1 290.2 %all-gather.9.cloned.1.call-start = ((), (), s32[]{:S(2)}) async-start(), calls=%async_computation.9 | async-start | bytes 1064960 | tf_op jit(solution)/shard_map/all_gather | solution.py:149
  123.8 386.4 %all-gather.7.cloned.1.call-start = ((), (), s32[]{:S(2)}) async-start(), calls=%async_computation.8 | async-start | bytes 1064960 | tf_op jit(solution)/shard_map/all_gather | solution.py:148
  124.6 482.6 %all-gather.11.cloned.1.call-start = ((), (), s32[]{:S(2)}) async-start(), calls=%async_computation.10 | async-start | bytes 1064960 | tf_op jit(solution)/shard_map/all_gather | solution.py:151
  125.1 1051.3 %reduce-scatter.3.cloned.1.call-start = ((), (), s32[]{:S(2)}) async-start(), calls=%async_computation.11 | async-start | bytes 2129920 | tf_op jit(solution)/shard_map/reduce_scatter | solution.py:194
  214.8 101.5 %copy-start.4 = (f32[1024]{0:T(1024)S(1)}, f32[1024]{0:T(1024)}, u32[]{:S(2)}) copy-start(f32[1024]{0:T(1024)} %param.23) | copy-start | bytes 12292
  607.1 3.0 copy-start.3
  610.1 0.8 copy-start.2
  610.6 3.5 copy-start.5
  623.6 1.4 copy-start.1
  627.4 1113.7 %reduce-scatter.5.cloned.1.call-start = ((), (), s32[]{:S(2)}) async-start(), calls=%async_computation.12 | async-start | bytes 2129920 | tf_op jit(solution)/shard_map/reduce_scatter | solution.py:195
  630.9 1229.4 %all-reduce.6.cloned.1.call-start = ((), (), s32[]{:S(2)}) async-start(), calls=%async_computation.13 | async-start | bytes 131072 | tf_op jit(solution)/shard_map/psum | solution.py:197
Sparse Core Ops, SparseCore 0:
  127.7 188.5 all-gather.4
  320.8 92.3 all-gather.8
  417.8 92.3 all-gather.6
  514.7 92.3 all-gather.10
  627.5 548.9 reduce-scatter.2
  1179.3 561.6 reduce-scatter.4
  1744.0 116.2 all-reduce.5
where the time goes:
time: 2160 us
  waiting for transfers between devices  1730 us (80%)
  blocking collectives  284 us (13%)
  starting transfers between devices  42.2 us (2%)
  matrix products  33.4 us (2%)
  local copies, waits for them, and re-layouts  27.3 us (1%)
    reduce_scatter x1, waiting for transfers between devices, per_device(): lax.psum_scatter(grad_out, 'member', scatter_dimension=0, tiled=True)  565 us
    reduce_scatter x1, waiting for transfers between devices, per_device(): lax.psum_scatter(grad_value, 'member', scatter_dimension=0, tiled=True)  546 us
    psum x1, blocking collectives, per_device(): squares = lax.psum(local_squares, 'member')  284 us
    psum x1, waiting for transfers between devices, per_device(): shard_value, shard_out = lax.psum((shard_value, shard_out), 'group')  119 us
    all_gather x1, waiting for transfers between devices, per_device(): lax.all_gather(w_value, 'member', axis=0, tiled=True)  99.9 us
    all_gather x1, waiting for transfers between devices, per_device(): lax.all_gather(w_query, 'member', axis=0, tiled=True)  90.9 us
    all_gather x1, waiting for transfers between devices, per_device(): lax.all_gather(w_key, 'member', axis=0, tiled=True)  90.9 us
    all_to_all x1, waiting for transfers between devices, per_device(): lax.all_to_all(sent_embed, 'member', split_axis=0, concat_axis=0, tiled=T...  82.5 us
  transfers between devices with their start and end apart: 12, of which 12 were waited for; matrix products, arithmetic and copies ran while one was open for 2% of the time, Pallas kernels for 0%

commit v1 on v0

v1 whole, which is shorter than its diff:
```python
import jax
import jax.numpy as jnp
from jax import lax
from jax.experimental import pallas as pl
from jax.experimental.pallas import tpu as pltpu
from jax.sharding import Mesh
from jax.sharding import PartitionSpec as P

AXES = ("g", "x", "zh", "y", "c")
SHAPE = (8, 4, 2, 4, 2)
SWAP = [(0, 1), (1, 0)]
FOUR_AWAY = [(g * 2 + zh, (g + 4) % 8 * 2 + 1 - zh) for g in range(8) for zh in range(2)]

HEADS = 4
HEAD_DIM = 128
ACTIONS = 18
STEPS = 24
BLOCKS = 8
BLOCK = 96
PAD = 24
TILES = 13

trace_lambda = 0.95
discount = 0.997
clip_norm = 1024.0

F32 = jnp.float32
BF16 = jnp.bfloat16
HIGHEST = lax.Precision.HIGHEST
VMEM = pl.BlockSpec(memory_space=pltpu.VMEM)
SMEM = pl.BlockSpec(memory_space=pltpu.SMEM)


def call(kernel, out_shape, in_specs, scratch=(), flops=0, moved=0, limit=32):
    return pl.pallas_call(
        kernel,
        out_shape=out_shape,
        in_specs=in_specs,
        out_specs=jax.tree.map(lambda s: VMEM, out_shape),
        scratch_shapes=list(scratch),
        compiler_params=pltpu.CompilerParams(vmem_limit_bytes=limit * 1024 * 1024),
        cost_estimate=pl.CostEstimate(flops=flops, bytes_accessed=moved, transcendentals=0),
    )


def shape(dims, dtype=F32):
    return jax.ShapeDtypeStruct(dims, dtype)


def iota(dims, axis):
    return lax.broadcasted_iota(jnp.int32, dims, axis)


def dot_nt(a, b):
    return lax.dot_general(a, b, (((1,), (1,)), ((), ())), preferred_element_type=F32)


def split(values):
    high = values.astype(BF16).astype(F32)
    return high, values - high


def step_of(lanes):
    out = lanes
    for edge in (24, 48, 72, 96, 120):
        out = out - jnp.where(lanes >= edge, 24, 0)
    return out


def payload_kernel(w_query, w_key, w_value, w_out, heads, out):
    for mat, ref in enumerate((w_query, w_key, w_value)):
        for tile in range(4):
            out[mat * 4 + tile] = ref[:, tile * 128 : (tile + 1) * 128]
    high, low = split(jnp.dot(w_out[...], heads[...], preferred_element_type=F32))
    both = high + pltpu.roll(low, 48, 1)
    out[12] = jnp.concatenate([both, jnp.zeros((8, 128), F32)], axis=0).astype(BF16)


def norm_kernel(embeds, gain, heads, normed, base, q_rows):
    turned = heads[...].astype(F32).T
    row = iota((128, 1024), 0)
    q_rows[...] = jnp.where(row >= 96, pltpu.roll(jnp.where(row < PAD, turned, 0.0), 96, 0), 0.0)
    both = turned[:48].astype(BF16)
    base[...] = jnp.zeros_like(base)
    for b in range(BLOCKS):
        rows = embeds[b * BLOCK : (b + 1) * BLOCK, :]
        values = rows.astype(F32)
        meansq = jnp.mean(values * values, axis=-1, keepdims=True)
        normed[b * BLOCK : (b + 1) * BLOCK, :] = (
            values * lax.rsqrt(meansq + 1e-06) * gain[...]
        ).astype(BF16)
        base[b, :, :BLOCK] = dot_nt(both, rows)


def pack_kernel(zh_ref, own, other, keep, recv, out):
    zh = zh_ref[0]
    high, low = split(keep[...] + recv[...])
    zeros = jnp.zeros((8, 128), F32)
    first = jnp.where(zh == 0, own[12].astype(F32), other[12].astype(F32))
    second = jnp.where(zh == 0, other[12], own[12])
    for d in range(16):
        for k in range(12):
            out[d, zh * TILES + k] = own[k]
            out[d, (1 - zh) * TILES + k] = other[k]
        at = 2 * d
        rows = [high[at : at + 1], low[at : at + 1], high[at + 1 : at + 2], low[at + 1 : at + 2]]
        table = jnp.concatenate([zeros] + rows + [zeros[:4]], axis=0)
        out[d, 12] = (first + table).astype(BF16)
        out[d, TILES + 12] = second


def main_kernel(
    c_ref, normed, base, mine, theirs, aux, out, value_rows,
    wall, wo, qkv, probs, mixed, logits, dq, grad_n, grad_g,
):
    c = c_ref[0]

    def unpack(s, total):
        x, y = s >> 2, s & 3
        for zh in range(2):
            for ref, core in ((mine, c), (theirs, 1 - c)):
                m = ((x * 2 + zh) * 4 + y) * 2 + core
                rows = pl.ds(pl.multiple_of(m * 16, 16), 16)
                for tile in range(12):
                    wall[rows, tile * 128 : (tile + 1) * 128] = ref[s, zh * TILES + tile]
                last = ref[s, zh * TILES + 12].astype(F32)
                wo[pl.ds(pl.multiple_of(m * 8, 8), 8), :] = last[:8]
                if zh == 0:
                    total = total + last
        return total

    total = lax.fori_loop(0, 16, unpack, jnp.zeros((16, 128), F32))
    weights = jnp.where(c == 0, total[8:9] + total[9:10], total[10:11] + total[11:12])

    turned = wo[...].T
    both = turned[:96].astype(BF16)
    own_value = turned[:PAD] + turned[48 : 48 + PAD]
    head_of = iota((PAD, 512), 1) >> 7
    for h in range(HEADS):
        value_rows[h * PAD : (h + 1) * PAD, :] = jnp.where(head_of == h, own_value, 0.0)
    value_rows[HEADS * PAD :, :] = jnp.zeros((128 - HEADS * PAD, 512), F32)

    def project(n, carry):
        cols = pl.ds(pl.multiple_of(n * 256, 256), 256)
        qkv[:, cols] = jnp.dot(
            normed[...], wall[:, cols], preferred_element_type=F32
        ).astype(BF16)
        return carry

    lax.fori_loop(0, 6, project, 0)

    row, col = iota((BLOCK, BLOCK), 0), iota((BLOCK, BLOCK), 1)
    row_step, col_step = step_of(row), step_of(col)
    causal = (row - row_step == col - col_step) & (col_step <= row_step)
    logits[...] = base[...]

    def attend(b, carry):
        rows = pl.ds(pl.multiple_of(b * BLOCK, 32), BLOCK)
        lengths = aux[3, pl.ds(b, 1), :][:, :BLOCK].astype(jnp.int32)
        allowed = causal & (col_step < lengths)
        for h in range(HEADS):
            at = h * HEAD_DIM
            scores = dot_nt(qkv[rows, at : at + 128], qkv[rows, 512 + at : 640 + at])
            scores = jnp.where(allowed, scores * HEAD_DIM ** (-0.5), -1e30)
            peak = jnp.max(scores, axis=-1, keepdims=True)
            grown = jnp.where(allowed, jnp.exp(scores - peak), 0.0)
            weighed = (grown / jnp.sum(grown, axis=-1, keepdims=True)).astype(BF16)
            probs[b * HEADS + h] = weighed
            mixed[rows, at : at + 128] = jnp.dot(
                weighed, qkv[rows, 1024 + at : 1152 + at], preferred_element_type=F32
            ).astype(BF16)
        lifted = dot_nt(both, mixed[rows, :])
        logits[b, :, :BLOCK] = logits[b, :, :BLOCK] + lifted[:48] + lifted[48:]
        return carry

    lax.fori_loop(0, BLOCKS, attend, 0)

    action_row = iota((BLOCKS, PAD, 128), 1)
    real = action_row < ACTIONS
    qvals = logits[:, :PAD, :]
    raised = jnp.where(real, logits[:, PAD:, :], -1e30)
    raised = jnp.where(real, jnp.exp(raised - jnp.max(raised, axis=1, keepdims=True)), 0.0)
    policy = raised / jnp.sum(raised, axis=1, keepdims=True)
    picked = action_row == aux[2].astype(jnp.int32)[:, None, :]
    values = jnp.sum(policy * qvals, axis=1)
    taken = jnp.sum(jnp.where(picked, qvals, 0.0), axis=1)
    chosen = jnp.sum(jnp.where(picked, policy, 0.0), axis=1)
    behaviour = aux[1]
    traces = trace_lambda * jnp.where(chosen >= behaviour, 1.0, chosen / behaviour)
    lengths = aux[3].astype(jnp.int32)
    lane, block = iota((BLOCKS, 128), 1), iota((BLOCKS, 128), 0)
    step = step_of(lane)
    onward = step + 1 < lengths

    def later(array, count):
        return pltpu.roll(array, 128 - count, 1)

    next_traces = later(traces, 1)
    targets = aux[0] + jnp.where(
        onward, discount * (later(values, 1) - next_traces * later(taken, 1)), 0.0
    )
    factor = jnp.where(onward, discount * next_traces, 0.0)
    for count in (1, 2, 4, 8, 16):
        targets = targets + factor * later(targets, count)
        factor = factor * later(factor, count)

    by_block = jnp.where(lane >> 2 == block, weights, 0.0)
    slot, place = iota((128, 128), 0), iota((128, 128), 1)
    spread = jnp.where((slot & 3) * STEPS == place - step_of(place), 1.0, 0.0)
    row_weight = jnp.dot(by_block, spread, preferred_element_type=F32, precision=HIGHEST)
    live = (step < lengths) & (row_weight != 0.0)
    errors = jnp.where(live, row_weight * (taken - targets), 0.0)
    high, low = split(errors)
    dq[:, :PAD, :] = jnp.where(picked, high[:, None, :], 0.0).astype(BF16)
    dq[:, PAD:, :] = jnp.where(picked, low[:, None, :], 0.0).astype(BF16)

    grad_n[...] = jnp.zeros_like(grad_n)
    grad_g[...] = jnp.zeros_like(grad_g)

    def backward(b, carry):
        rows = pl.ds(pl.multiple_of(b * BLOCK, 32), BLOCK)
        given = dq[b][:, :BLOCK]
        parts = []
        for h in range(HEADS):
            both_parts = jnp.dot(given, probs[b * HEADS + h], preferred_element_type=F32)
            parts.append(both_parts[:PAD] + both_parts[PAD:])
        high, low = split(jnp.concatenate(parts, axis=0))
        stacked = jnp.concatenate([high, low], axis=0).astype(BF16)
        update = jnp.dot(stacked, normed[rows, :], preferred_element_type=F32)
        grad_n[:96, :] += update[:96] + update[96:]
        update = jnp.dot(given, mixed[rows, :], preferred_element_type=F32)
        grad_g[96 : 96 + PAD, :] += update[:PAD] + update[PAD:]
        return carry

    lax.fori_loop(0, BLOCKS, backward, 0)

    by_row, by_feature = grad_n[...].T, grad_g[...].T
    for p in range(32):
        x, y, core = p >> 3, (p >> 1) & 3, p & 1
        m0 = (x * 8 + y) * 2 + core
        m1 = m0 + 8
        upper = by_row[m0 * 16 : m0 * 16 + 16] + jnp.concatenate(
            [by_feature[m0 * 8 : m0 * 8 + 8], by_feature[m1 * 8 : m1 * 8 + 8]], axis=0
        )
        out[p] = jnp.concatenate([upper, by_row[m1 * 16 : m1 * 16 + 16]], axis=0).astype(out.dtype)


def grads_kernel(parts, value_rows, q_rows, grad_value, grad_out, squares):
    total = parts[0].astype(F32)
    for z in range(1, 16):
        total = total + parts[z].astype(F32)
    by_value = jnp.dot(total, value_rows[...], preferred_element_type=F32, precision=HIGHEST)
    by_out = jnp.dot(total[:16], q_rows[...], preferred_element_type=F32, precision=HIGHEST)
    grad_value[...] = by_value
    grad_out[...] = by_out
    sums = jnp.zeros((8, 128), F32)
    for array in (by_value * by_value, by_out * by_out):
        for r in range(0, array.shape[0], 8):
            for k in range(0, array.shape[1], 128):
                sums = sums + array[r : r + 8, k : k + 128]
    squares[...] = sums


def clip_kernel(zh_ref, squares, by_value, by_out, grad_value, grad_out):
    zh = zh_ref[0]
    total = jnp.sum(jnp.sum(squares[...], axis=0), keepdims=True)
    scale = jnp.minimum(1.0, clip_norm / jnp.sqrt(total))
    grad_value[...] = by_value[pl.ds(pl.multiple_of(zh * 16, 16), 16), :] * scale
    grad_out[...] = by_out[pl.ds(pl.multiple_of(zh * 8, 8), 8), :] * scale


def make_payload(w_query, w_key, w_value, w_out, heads):
    return call(payload_kernel, shape((TILES, 16, 128), BF16), [VMEM] * 5, flops=2 * 10**6, moved=10**5)(
        w_query, w_key, w_value, w_out, heads
    )


def make_normed(embeds, gain, heads):
    return call(
        norm_kernel,
        (shape((768, 1024), BF16), shape((BLOCKS, 48, 128)), shape((128, 1024))),
        [VMEM] * 3,
        flops=10**8,
        moved=4 * 10**6,
    )(embeds, gain, heads)


def make_message(zh, own, other, keep, recv):
    return call(
        pack_kernel, shape((16, 2 * TILES, 16, 128), BF16), [SMEM] + [VMEM] * 4, moved=2 * 10**6
    )(zh, own, other, keep, recv)


def make_sums(core, normed, base, mine, theirs, aux, dtype):
    return call(
        main_kernel,
        (shape((32, 32, 128), dtype), shape((128, 512))),
        [SMEM] + [VMEM] * 5,
        [
            pltpu.VMEM((1024, 1536), BF16),
            pltpu.VMEM((512, 128), F32),
            pltpu.VMEM((768, 1536), BF16),
            pltpu.VMEM((BLOCKS * HEADS, BLOCK, BLOCK), BF16),
            pltpu.VMEM((768, 512), BF16),
            pltpu.VMEM((BLOCKS, 48, 128), F32),
            pltpu.VMEM((BLOCKS, 48, 128), BF16),
            pltpu.VMEM((128, 1024), F32),
            pltpu.VMEM((128, 512), F32),
        ],
        flops=4 * 10**9,
        moved=10**7,
        limit=48,
    )(core, normed, base, mine, theirs, aux)


def make_grads(parts, value_rows, q_rows):
    return call(
        grads_kernel,
        (shape((32, 512)), shape((16, 1024)), shape((8, 128))),
        [VMEM] * 3,
        flops=10**7,
        moved=10**6,
    )(parts, value_rows, q_rows)


def make_clipped(zh, squares, by_value, by_out):
    return call(
        clip_kernel, (shape((16, 512)), shape((8, 1024))), [SMEM] + [VMEM] * 3, moved=2 * 10**5
    )(zh, squares, by_value, by_out)


def padded_heads(q_head, policy_head):
    width = ((0, 0), (0, PAD - ACTIONS))
    return jnp.concatenate(
        [jnp.pad(q_head, width), jnp.pad(policy_head, width), jnp.zeros((1024, 80), BF16)], axis=1
    )


def row_facts(replay_steps, replay_actions, replay_lengths):
    def lanes(array, fill):
        flat = array.astype(F32).reshape(BLOCKS, BLOCK)
        return jnp.pad(flat, ((0, 0), (0, 128 - BLOCK)), constant_values=fill)

    lengths = jnp.broadcast_to(replay_lengths[:, None], (32, STEPS))
    return jnp.stack([
        lanes(replay_steps[:, 0, :], 0.0),
        lanes(replay_steps[:, 1, :], 1.0),
        lanes(replay_actions, 0.0),
        lanes(lengths, 0.0),
    ])


def slot_weights(sample_owner, sample_slot, sample_weight, zh):
    owner = sample_owner[:, 0]
    place = (owner >> 4) * 8 + (owner & 7)
    half = (owner >> 3) & 1
    hit = (place[:, None, None] == jnp.arange(32)[None, :, None]) & (
        sample_slot[:, None, None] == jnp.arange(128)[None, None, :]
    )
    weights = jnp.where(hit, sample_weight[:, None, None], 0.0)
    stays = (half == zh)[:, None, None]
    return jnp.sum(jnp.where(stays, weights, 0.0), axis=0), jnp.sum(jnp.where(stays, 0.0, weights), axis=0)


def per_device(
    replay_embed,
    replay_steps,
    replay_actions,
    replay_lengths,
    sample_owner,
    sample_slot,
    sample_weight,
    norm_gain,
    w_query,
    w_key,
    w_value,
    w_out,
    q_head,
    policy_head,
):
    zh = lax.axis_index("zh").astype(jnp.int32)
    core = lax.axis_index("c").astype(jnp.int32)
    heads = padded_heads(q_head, policy_head)
    own = make_payload(w_query, w_key, w_value, w_out, heads)
    other = lax.ppermute(own, ("g", "zh"), FOUR_AWAY)
    keep, send = slot_weights(sample_owner, sample_slot, sample_weight, zh)
    recv = lax.ppermute(send, "zh", SWAP)
    normed, base, q_rows = make_normed(
        replay_embed.reshape(768, 1024), norm_gain.reshape(1, 1024), heads
    )
    aux = row_facts(replay_steps, replay_actions, replay_lengths)
    message = make_message(zh.reshape(1), own, other, keep, recv)
    mine = lax.all_to_all(message, ("x", "y"), split_axis=0, concat_axis=0, tiled=True)
    theirs = lax.ppermute(mine, "c", SWAP)
    sums, value_rows = make_sums(core.reshape(1), normed, base, mine, theirs, aux, F32)
    parts = lax.all_to_all(sums, ("x", "y", "c"), split_axis=0, concat_axis=0, tiled=True)
    plane = jnp.sum(parts.astype(F32), axis=0)
    copies = jnp.broadcast_to(plane[None], (16, 32, 128))
    planes = lax.all_to_all(copies, ("zh", "g"), split_axis=0, concat_axis=0, tiled=True)
    by_value, by_out, squares = make_grads(planes, value_rows, q_rows)
    squares = lax.all_to_all(
        jnp.broadcast_to(squares[None], (32, 8, 128)), ("x", "y", "c"), split_axis=0, concat_axis=0, tiled=True
    )
    return make_clipped(zh.reshape(1), squares, by_value, by_out)


def solution(mesh):
    fine = Mesh(mesh.devices.reshape(SHAPE), AXES)
    rows, member = AXES, AXES[1:]
    return jax.shard_map(
        per_device,
        mesh=fine,
        in_specs=(
            P(rows, None, None),
            P(rows, None, None),
            P(rows, None),
            P(rows),
            P(rows, None),
            P(rows),
            P(rows),
            P(),
            P(member, None),
            P(member, None),
            P(member, None),
            P(member, None),
            P(),
            P(),
        ),
        out_specs=(P(member, None), P(member, None)),
        check_vma=False,
    )
```

time: 2160 us -> 154 us (0.07)
  waiting for transfers between devices: 1730 us -> 8.44 us
  blocking collectives: 284 us -> 79.6 us
  matrix products: 33.4 us -> 0 us
  Pallas kernels: 0 us -> 24.7 us
    reduce_scatter x2 -> x0, waiting for transfers between devices: 1110 us -> none  [the longest x1 565 us: per_device(): lax.psum_scatter(grad_out, 'member', scatter_dimension=0, tiled=True)]
    all_gather x4 -> x0, waiting for transfers between devices: 364 us -> none  [the longest x1 99.9 us: per_device(): lax.all_gather(w_value, 'member', axis=0, tiled=True)]
    psum x1 -> x0, blocking collectives: 284 us -> none  [per_device(): squares = lax.psum(local_squares, 'member')]
    all_to_all x5 -> x0, waiting for transfers between devices: 138 us -> none  [the longest x1 82.5 us: per_device(): lax.all_to_all(sent_embed, 'member', split_axis=0, concat_axis=0, tiled=T...]
    psum x1 -> x0, waiting for transfers between devices: 119 us -> none  [per_device(): shard_value, shard_out = lax.psum((shard_value, shard_out), 'group')]
    all_to_all x0 -> x4, blocking collectives: none -> 79.6 us  [the longest x1 28.4 us: per_device(): lax.all_to_all(message, ('x', 'y'), split_axis=0, concat_axis=0, tiled=True)]
    all_to_all x5 -> x0, starting transfers between devices: 41.9 us -> none  [the longest x1 22.2 us: per_device(): lax.all_to_all(wanted, 'member', split_axis=0, concat_axis=0, tiled=True)]
    dot_general x12 -> x0, matrix products: 29.8 us -> none  [the longest x3 10.9 us: project(): jnp.dot(normed, matrix, preferred_element_type=jnp.float32)]
  transfers between devices with their start and end apart: 12 -> 3, of which waited for: 12 -> 1; matrix products, arithmetic and copies ran while one was open for 2% -> 6% of each run, Pallas kernels for 0% -> 1%
where the time goes in v1:
time: 154 us; the launch traced here: 153 us
  blocking collectives  79.6 us (52%)
  Pallas kernels  24.7 us (16%)
  starting transfers between devices  23.4 us (15%)
  local copies, waits for them, and re-layouts  14.2 us (9%)
  waiting for transfers between devices  8.44 us (5%)
    all_to_all x1, blocking collectives, per_device(): lax.all_to_all(message, ('x', 'y'), split_axis=0, concat_axis=0, tiled=True)  28.4 us
    pallas_call x1, Pallas kernels, make_sums(): call(main_kernel, (shape((32, 32, 128), dtype), shape((128, 512))), [SMEM...  21.9 us
    all_to_all x1, blocking collectives, per_device(): lax.all_to_all(copies, ('zh', 'g'), split_axis=0, concat_axis=0, tiled=True)  20.8 us
    all_to_all x1, blocking collectives, per_device(): lax.all_to_all(sums, ('x', 'y', 'c'), split_axis=0, concat_axis=0, tiled=...  15.3 us
    all_to_all x1, blocking collectives, per_device(): lax.all_to_all(jnp.broadcast_to(squares[None], (32, 8, 128)), ('x', 'y',...  15.1 us
    ppermute x1, starting transfers between devices, per_device(): other = lax.ppermute(own, ('g', 'zh'), FOUR_AWAY)  13.3 us
    ppermute x1, waiting for transfers between devices, per_device(): recv = lax.ppermute(send, 'zh', SWAP)  8.43 us
    unnamed x34, local copies, waits for them, and re-layouts  5.7 us
  transfers between devices with their start and end apart: 3, of which 1 were waited for; matrix products, arithmetic and copies ran while one was open for 6% of the time, Pallas kernels for 1%

profile of v1, /device:TPU:1, one launch (start us, length us, event | category | flops | bytes accessed | tf_op | source)
XLA Modules:
  0.0 152.7 jit_solution(15063001987693114072)
XLA Ops:
  0.6 0.0 copy-start.14
  0.6 0.0 copy-start.13
  0.7 0.0 copy-start.12
  0.7 1.0 copy.26
  1.7 1.0 copy.27
  2.7 0.1 pad.34.clone
  2.7 0.2 fusion.6.heads
  3.0 0.0 copy-start.3
  3.0 0.7 copy-done.3
  3.7 0.0 copy-start.4
  3.7 0.7 copy-done.4
  4.4 0.0 copy-start.5
  4.4 0.7 copy-done.5
  5.1 0.7 copy-done.6
  5.8 0.2 shard_map.150.own
  6.1 13.3 %collective-permute-start = (bf16[13,16,128]{2,1,0:T(8,128)(2,1)S(1)}, bf16[13,16,128]{2,1,0:T(8,128)(2,1)S(1)}, u32[]{:S(2)}, u32[]{:S(2)}) collective-permute-start(bf16[13,16,128]{2,1,0:T(8,128)(2,1)S(1)} %shard_map.150.own), channel_id=1, source_target_pairs={{0,264},{8,256},{64,328},{72,320},{128,392},{136,384},{192,456},{2... | collective-permute-start | bytes 159752 | tf_op jit(solution)/shard_map/ppermute | solution.py:385
  19.4 0.0 copy-done.14
  19.4 0.1 iota_compare_fusion.4
  19.5 0.0 copy-done.13
  19.5 0.1 iota_compare_fusion.3
  19.5 0.0 copy-done.12
  19.5 0.3 fusion.1
  19.8 4.9 %collective-permute-start.1 = (f32[32,128]{1,0:T(8,128)S(1)}, f32[32,128]{1,0:T(8,128)S(1)}, u32[]{:S(2)}, u32[]{:S(2)}) collective-permute-start(f32[32,128]{1,0:T(8,128)S(1)} %get-tuple-element.18), channel_id=1, source_target_pairs={{0,8},{8,0},{1,9},{9,1},{2,10},{10,2},{3,11},{11,3},{4,12},{12,4},... | collective-permute-start | bytes 49160 | tf_op jit(solution)/shard_map/ppermute | solution.py:387
  24.8 8.4 %collective-permute-done.1.recv = f32[32,128]{1,0:T(8,128)S(1)} collective-permute-done((f32[32,128]{1,0:T(8,128)S(1)}, f32[32,128]{1,0:T(8,128)S(1)}, u32[]{:S(2)}, u32[]{:S(2)}) %collective-permute-start.1) | collective-permute-done | bytes 16416 | tf_op jit(solution)/shard_map/ppermute | solution.py:387
  33.2 0.0 collective-permute-done.other
  33.2 0.2 shard_map.151
  33.4 0.0 copy-start.15
  33.4 0.0 copy-start
  33.5 0.0 copy-start.7
  33.5 28.4 %all_to_all.20.mine = bf16[16,26,16,128]{3,2,1,0:T(8,128)(2,1)S(1)} all-to-all(bf16[16,26,16,128]{3,2,1,0:T(8,128)(2,1)S(1)} %shard_map.151), channel_id=1, replica_groups=mesh['g'=8,'x'=4,'zh'=2,'y'=4,'c'=2] {'x','y'}, dimensions={0} | all-to-all | bytes 3407872 | tf_op jit(solution)/shard_map/all_to_all | solution.py:393
  61.9 5.3 %collective-permute-start.2 = (bf16[16,26,16,128]{3,2,1,0:T(8,128)(2,1)S(1)}, bf16[16,26,16,128]{3,2,1,0:T(8,128)(2,1)}, u32[]{:S(2)}, u32[]{:S(2)}) collective-permute-start(bf16[16,26,16,128]{3,2,1,0:T(8,128)(2,1)S(1)} %all_to_all.20.mine), channel_id=1, source_target_pairs={{0,1},{1,0},{2,3},{3,2},{4,5},{5,4},{6,7},{7,6},{8,9},{9,8},{10,11... | collective-permute-start | bytes 5111816 | tf_op jit(solution)/shard_map/ppermute | solution.py:394
  67.1 0.0 copy-done.15
  67.2 0.1 broadcast_in_dim.65
  67.2 0.7 broadcast_in_dim.66
  67.9 1.4 broadcast_in_dim.67
  69.3 0.7 convert_element_type.22
  70.0 0.7 copy.30
  70.7 0.0 copy-start.8
  70.7 1.4 reshape.115
  72.1 1.3 fusion.7
  73.4 0.8 copy.28
  74.1 0.7 convert_element_type.20
  74.8 0.8 copy.29
  75.6 0.7 convert_element_type.21
  76.3 0.0 copy-start.9
  76.3 0.0 copy-start.10
  76.3 0.0 copy-done
  76.3 0.0 copy-done.7
  76.3 1.1 shard_map.149
  77.4 0.0 copy-start.1
  77.4 0.8 copy-done.1
  78.2 0.0 copy-done.8
  78.2 0.0 copy-done.9
  78.2 0.0 copy-done.10
  78.2 0.0 copy-done.11
  78.2 0.0 collective-permute-done.2.theirs
  78.2 21.9 %shard_map.152 = (f32[32,32,128]{2,1,0:T(8,128)S(1)}, f32[128,512]{1,0:T(8,128)S(1)}) custom-call(s32[1]{0:T(128)} %bitcast.1.c_ref, bf16[768,1024]{1,0:T(8,128)(2,1)S(1)} %get-tuple-element.10.normed, f32[8,48,128]{2,1,0:T(8,128)S(1)} %get-tuple-element.11.base, bf16[16,26,16,128]{3,2,1,0:T(8,128)(2,1)S(1)} %all_to_all.20.mine, ...), custom_call_target="tpu_custom_call" | custom-call | flops 4000000000 | bytes 10000000 | tf_op jit(solution)/shard_map/pallas_call | solution.py:295
  100.1 0.0 copy-start.2
  100.1 15.3 %all_to_all.21 = f32[32,32,128]{2,1,0:T(8,128)S(1)} all-to-all(f32[32,32,128]{2,1,0:T(8,128)S(1)} %get-tuple-element.12), channel_id=1, replica_groups=mesh['g'=8,'x'=4,'zh'=2,'y'=4,'c'=2] {'x','y','c'}, dimensions={0} | all-to-all | bytes 1048576 | tf_op jit(solution)/shard_map/all_to_all | solution.py:396
  115.6 20.8 %all_to_all.22.parts = f32[16,32,128]{2,1,0:T(8,128)S(1)} all-to-all(f32[16,32,128]{2,1,0:T(8,128)S(1)} %broadcast_in_dim.68), channel_id=1, replica_groups=mesh['g'=8,'x'=4,'zh'=2,'y'=4,'c'=2] {'zh','g'}, dimensions={0} | all-to-all | bytes 524288 | tf_op jit(solution)/shard_map/all_to_all | solution.py:399
  136.3 0.0 copy-done.2
  136.3 0.5 shard_map.153
  136.9 15.1 %all_to_all.23.squares = f32[32,8,128]{2,1,0:T(8,128)S(1)} all-to-all(f32[32,8,128]{2,1,0:T(8,128)S(1)} %broadcast_in_dim.69), channel_id=1, replica_groups=mesh['g'=8,'x'=4,'zh'=2,'y'=4,'c'=2] {'x','y','c'}, dimensions={0} | all-to-all | bytes 262144 | tf_op jit(solution)/shard_map/all_to_all | solution.py:401
  151.9 0.8 shard_map.154
  (12 shorter events, 0.1 us)
Async XLA Ops:
  0.6 18.7 %copy-start.14 = (s32[32,1]{0,1:T(1,128)S(1)}, s32[32,1]{0,1:T(1,128)}, u32[]{:S(2)}) copy-start(s32[32,1]{0,1:T(1,128)} %param.18) | copy-start | bytes 388
  0.6 18.8 %copy-start.13 = (s32[32]{0:T(128)S(1)}, s32[32]{0:T(128)}, u32[]{:S(2)}) copy-start(s32[32]{0:T(128)} %param.19) | copy-start | bytes 388
  0.7 18.9 %copy-start.12 = (f32[32]{0:T(128)S(1)}, f32[32]{0:T(128)}, u32[]{:S(2)}) copy-start(f32[32]{0:T(128)} %param.20) | copy-start | bytes 388
  3.0 0.7 copy-start.3
  3.7 0.7 copy-start.4
  4.4 0.7 copy-start.5
  5.1 0.7 copy-start.6
  6.1 27.1 %collective-permute-start = (bf16[13,16,128]{2,1,0:T(8,128)(2,1)S(1)}, bf16[13,16,128]{2,1,0:T(8,128)(2,1)S(1)}, u32[]{:S(2)}, u32[]{:S(2)}) collective-permute-start(bf16[13,16,128]{2,1,0:T(8,128)(2,1)S(1)} %shard_map.150.own), channel_id=1, source_target_pairs={{0,264},{8,256},{64,328},{72,320},{128,392},{136,384},{192,456},{2... | collective-permute-start | bytes 159752 | tf_op jit(solution)/shard_map/ppermute | solution.py:385
  19.8 13.3 %collective-permute-start.1 = (f32[32,128]{1,0:T(8,128)S(1)}, f32[32,128]{1,0:T(8,128)S(1)}, u32[]{:S(2)}, u32[]{:S(2)}) collective-permute-start(f32[32,128]{1,0:T(8,128)S(1)} %get-tuple-element.18), channel_id=1, source_target_pairs={{0,8},{8,0},{1,9},{9,1},{2,10},{10,2},{3,11},{11,3},{4,12},{12,4},... | collective-permute-start | bytes 49160 | tf_op jit(solution)/shard_map/ppermute | solution.py:387
  33.4 33.7 %copy-start.15 = (s32[32]{0:T(128)S(1)}, s32[32]{0:T(128)}, u32[]{:S(2)}) copy-start(s32[32]{0:T(128)} %param.17) | copy-start | bytes 388
  33.4 42.8 %copy-start = (bf16[32,24,1024]{2,1,0:T(8,128)(2,1)S(1)}, bf16[32,24,1024]{2,1,0:T(8,128)(2,1)}, u32[]{:S(2)}) copy-start(bf16[32,24,1024]{2,1,0:T(8,128)(2,1)} %param.14) | copy-start | bytes 4718596
  33.5 42.8 %copy-start.7 = (f32[1024]{0:T(1024)S(1)}, f32[1024]{0:T(1024)}, u32[]{:S(2)}) copy-start(f32[1024]{0:T(1024)} %param.21) | copy-start | bytes 12292
  61.9 16.4 %collective-permute-start.2 = (bf16[16,26,16,128]{3,2,1,0:T(8,128)(2,1)S(1)}, bf16[16,26,16,128]{3,2,1,0:T(8,128)(2,1)}, u32[]{:S(2)}, u32[]{:S(2)}) collective-permute-start(bf16[16,26,16,128]{3,2,1,0:T(8,128)(2,1)S(1)} %all_to_all.20.mine), channel_id=1, source_target_pairs={{0,1},{1,0},{2,3},{3,2},{4,5},{5,4},{6,7},{7,6},{8,9},{9,8},{10,11... | collective-permute-start | bytes 5111816 | tf_op jit(solution)/shard_map/ppermute | solution.py:394
  70.7 7.5 %copy-start.8 = (f32[8,96]{1,0:T(8,128)S(1)}, f32[8,96]{1,0:T(8,128)}, u32[]{:S(2)}) copy-start(f32[8,96]{1,0:T(8,128)} %broadcast_in_dim.67) | copy-start | bytes 9220
  76.3 1.9 %copy-start.9 = (f32[8,96]{1,0:T(8,128)S(1)}, f32[8,96]{1,0:T(8,128)}, u32[]{:S(2)}) copy-start(f32[8,96]{1,0:T(8,128)} %reshape.115) | copy-start | bytes 9220
  76.3 1.9 %copy-start.10 = (bf16[8,96]{1,0:T(8,128)(2,1)S(1)}, bf16[8,96]{1,0:T(8,128)(2,1)}, u32[]{:S(2)}) copy-start(bf16[8,96]{1,0:T(8,128)(2,1)} %convert_element_type.20) | copy-start | bytes 4612
  76.3 1.9 %copy-start.11 = (bf16[8,96]{1,0:T(8,128)(2,1)S(1)}, bf16[8,96]{1,0:T(8,128)(2,1)}, u32[]{:S(2)}) copy-start(bf16[8,96]{1,0:T(8,128)(2,1)} %convert_element_type.21) | copy-start | bytes 4612
  77.4 0.8 copy-start.1
  100.1 36.2 %copy-start.2 = (f32[128,1024]{1,0:T(8,128)S(1)}, f32[128,1024]{1,0:T(8,128)}, u32[]{:S(2)}) copy-start(f32[128,1024]{1,0:T(8,128)} %copy-done.1) | copy-start | bytes 1572868

commit v2 on v1

--- a/solution.py
+++ b/solution.py
@@ -9,7 +9,6 @@
 AXES = ("g", "x", "zh", "y", "c")
 SHAPE = (8, 4, 2, 4, 2)
 SWAP = [(0, 1), (1, 0)]
-FOUR_AWAY = [(g * 2 + zh, (g + 4) % 8 * 2 + 1 - zh) for g in range(8) for zh in range(2)]
 
 HEADS = 4
 HEAD_DIM = 128
@@ -28,10 +27,11 @@
 BF16 = jnp.bfloat16
 HIGHEST = lax.Precision.HIGHEST
 VMEM = pl.BlockSpec(memory_space=pltpu.VMEM)
+HBM = pl.BlockSpec(memory_space=pltpu.HBM)
 SMEM = pl.BlockSpec(memory_space=pltpu.SMEM)
 
 
-def call(kernel, out_shape, in_specs, scratch=(), flops=0, moved=0, limit=32):
+def call(kernel, out_shape, in_specs, scratch=(), flops=0, moved=0, limit=10):
     return pl.pallas_call(
         kernel,
         out_shape=out_shape,
@@ -67,20 +67,74 @@
     return out
 
 
-def payload_kernel(w_query, w_key, w_value, w_out, heads, out):
-    for mat, ref in enumerate((w_query, w_key, w_value)):
-        for tile in range(4):
-            out[mat * 4 + tile] = ref[:, tile * 128 : (tile + 1) * 128]
-    high, low = split(jnp.dot(w_out[...], heads[...], preferred_element_type=F32))
+def stacked_heads(q_turned, policy_turned, rows):
+    gap = jnp.zeros((PAD - ACTIONS, 1024), F32)
+    parts = [q_turned[...].astype(F32), gap, policy_turned[...].astype(F32), gap]
+    if rows > 2 * PAD:
+        parts.append(jnp.zeros((rows - 2 * PAD, 1024), F32))
+    return jnp.concatenate(parts, axis=0).astype(BF16)
+
+
+def payload_kernel(
+    zh_ref, w_query_at, w_key_at, w_value_at, w_out_at, q_at, policy_at, owner_at, slot_at, weight_at,
+    own, copies, keep,
+    w_query, w_key, w_value, w_out, q_turned, policy_turned, owner, slot, weight, sems,
+):
+    pairs = (
+        (w_query_at, w_query), (w_key_at, w_key), (w_value_at, w_value),
+        (w_out_at, w_out), (q_at, q_turned), (policy_at, policy_turned),
+        (owner_at, owner), (slot_at, slot), (weight_at, weight),
+    )
+    moves = [pltpu.make_async_copy(a, b, sems.at[k]) for k, (a, b) in enumerate(pairs)]
+    for move in moves:
+        move.start()
+    for move in moves:
+        move.wait()
+    heads = stacked_heads(q_turned, policy_turned, 128)
+    high, low = split(dot_nt(w_out[...], heads))
     both = high + pltpu.roll(low, 48, 1)
-    out[12] = jnp.concatenate([both, jnp.zeros((8, 128), F32)], axis=0).astype(BF16)
-
-
-def norm_kernel(embeds, gain, heads, normed, base, q_rows):
-    turned = heads[...].astype(F32).T
-    row = iota((128, 1024), 0)
-    q_rows[...] = jnp.where(row >= 96, pltpu.roll(jnp.where(row < PAD, turned, 0.0), 96, 0), 0.0)
-    both = turned[:48].astype(BF16)
+    last = jnp.concatenate([both, jnp.zeros((8, 128), F32)], axis=0).astype(BF16)
+    tiles = [
+        ref[:, tile * 128 : (tile + 1) * 128] for ref in (w_query, w_key, w_value) for tile in range(4)
+    ] + [last]
+    for k, tile in enumerate(tiles):
+        own[k] = tile
+        for d in range(16):
+            copies[d, k] = tile
+
+    member = owner[...]
+    code = ((member >> 4) * 8 + (member & 7)) * 32 + slot[...]
+    stays = ((member >> 3) & 1) == zh_ref[0]
+    diagonal = iota((32, 32), 0) == iota((32, 32), 1)
+
+    def column(lanes):
+        return jnp.sum(jnp.where(diagonal, lanes, 0.0), axis=1, keepdims=True)
+
+    at = column(code.astype(F32)).astype(jnp.int32)
+    by_row = jnp.where(at >> 7 == iota((32, 8), 1), 1.0, 0.0)
+    place = (at & 127) == iota((32, 128), 1)
+
+    def table(weights):
+        return lax.dot_general(
+            by_row,
+            jnp.where(place, column(weights), 0.0),
+            (((0,), (0,)), ((), ())),
+            preferred_element_type=F32,
+            precision=HIGHEST,
+        )
+
+    keep[...] = table(jnp.where(stays, weight[...], 0.0))
+    high, low = split(table(jnp.where(stays, 0.0, weight[...])))
+    own[TILES] = jnp.concatenate([high, low], axis=0).astype(BF16)
+
+
+def norm_kernel(
+    embeds, gain, q_turned, policy_turned, steps, actions, lengths, normed, base, q_rows, aux
+):
+    both = stacked_heads(q_turned, policy_turned, 48)
+    q_rows[...] = jnp.concatenate(
+        [jnp.zeros((96, 1024), F32), both[:PAD].astype(F32), jnp.zeros((8, 1024), F32)], axis=0
+    )
     base[...] = jnp.zeros_like(base)
     for b in range(BLOCKS):
         rows = embeds[b * BLOCK : (b + 1) * BLOCK, :]
@@ -91,46 +145,76 @@
         ).astype(BF16)
         base[b, :, :BLOCK] = dot_nt(both, rows)
 
-
-def pack_kernel(zh_ref, own, other, keep, recv, out):
-    zh = zh_ref[0]
-    high, low = split(keep[...] + recv[...])
-    zeros = jnp.zeros((8, 128), F32)
-    first = jnp.where(zh == 0, own[12].astype(F32), other[12].astype(F32))
-    second = jnp.where(zh == 0, other[12], own[12])
+    place = iota((STEPS, 128), 1)
+    by_step = jnp.where(step_of(place) == iota((STEPS, 128), 0), 1.0, 0.0).astype(BF16)
+    seq, lane = iota((32, 128), 0), iota((32, 128), 1)
+    real = (seq & 3) * STEPS == lane - step_of(lane)
+    block, member = iota((BLOCKS, 32), 0), iota((BLOCKS, 32), 1)
+    by_block = jnp.where(member >> 2 == block, 1.0, 0.0)
+
+    def lanes(array):
+        wide = lax.dot_general(
+            array.astype(BF16), by_step, (((0,), (0,)), ((), ())), preferred_element_type=F32
+        )
+        return fold(jnp.where(real, wide, 0.0))
+
+    def fold(wide):
+        return jnp.dot(by_block.astype(BF16), wide.astype(BF16), preferred_element_type=F32)
+
+    aux[0] = lanes(steps[0])
+    aux[1] = jnp.where(iota((BLOCKS, 128), 1) >= BLOCK, 1.0, lanes(steps[1]))
+    aux[2] = lanes(actions[...].astype(F32))
+    shares = by_block * lengths[...].astype(F32)
+    aux[3] = jnp.dot(
+        shares.astype(BF16), jnp.where(real, 1.0, 0.0).astype(BF16), preferred_element_type=F32
+    )
+
+
+def pack_kernel(other, keep_at, out, keep, sem):
+    move = pltpu.make_async_copy(keep_at, keep, sem)
+    move.start()
     for d in range(16):
         for k in range(12):
-            out[d, zh * TILES + k] = own[k]
-            out[d, (1 - zh) * TILES + k] = other[k]
-        at = 2 * d
-        rows = [high[at : at + 1], low[at : at + 1], high[at + 1 : at + 2], low[at + 1 : at + 2]]
-        table = jnp.concatenate([zeros] + rows + [zeros[:4]], axis=0)
-        out[d, 12] = (first + table).astype(BF16)
-        out[d, TILES + 12] = second
+            out[d, k] = other[k]
+    move.wait()
+    table = other[TILES].astype(F32)
+    high, low = split(keep[...] + table[:8] + table[8:])
+    zeros = jnp.zeros((8, 128), F32)
+    last = other[12].astype(F32)
+    for d in range(16):
+        rows = jnp.concatenate(
+            [high[d >> 1 : (d >> 1) + 1], low[d >> 1 : (d >> 1) + 1], zeros[:6]], axis=0
+        )
+        if d & 1:
+            rows = pltpu.roll(rows, 64, 1)
+        out[d, 12] = (last + jnp.concatenate([zeros, rows], axis=0)).astype(BF16)
 
 
 def main_kernel(
-    c_ref, normed, base, mine, theirs, aux, out, value_rows,
+    place, normed, base, mine_first, theirs_first, mine_last, theirs_last, aux, out, value_rows,
     wall, wo, qkv, probs, mixed, logits, dq, grad_n, grad_g,
 ):
-    c = c_ref[0]
+    zh, c = place[0], place[1]
+    sources = (
+        (mine_first, zh, c), (theirs_first, zh, 1 - c), (mine_last, 1 - zh, c), (theirs_last, 1 - zh, 1 - c)
+    )
 
     def unpack(s, total):
         x, y = s >> 2, s & 3
-        for zh in range(2):
-            for ref, core in ((mine, c), (theirs, 1 - c)):
-                m = ((x * 2 + zh) * 4 + y) * 2 + core
-                rows = pl.ds(pl.multiple_of(m * 16, 16), 16)
-                for tile in range(12):
-                    wall[rows, tile * 128 : (tile + 1) * 128] = ref[s, zh * TILES + tile]
-                last = ref[s, zh * TILES + 12].astype(F32)
-                wo[pl.ds(pl.multiple_of(m * 8, 8), 8), :] = last[:8]
-                if zh == 0:
-                    total = total + last
+        for k, (source, half, core) in enumerate(sources):
+            m = ((x * 2 + half) * 4 + y) * 2 + core
+            rows = pl.ds(pl.multiple_of(m * 16, 16), 16)
+            for tile in range(12):
+                wall[rows, tile * 128 : (tile + 1) * 128] = source[s, tile]
+            last = source[s, 12].astype(F32)
+            wo[pl.ds(pl.multiple_of(m * 8, 8), 8), :] = last[:8]
+            if k >= 2:
+                total = total + last
         return total
 
-    total = lax.fori_loop(0, 16, unpack, jnp.zeros((16, 128), F32))
-    weights = jnp.where(c == 0, total[8:9] + total[9:10], total[10:11] + total[11:12])
+    total = lax.fori_loop(0, 16, unpack, jnp.zeros((16, 128), F32), unroll=2)
+    weights = total[8:9] + total[9:10]
+    weights = jnp.where(c == 0, weights, pltpu.roll(weights, 96, 1))
 
     turned = wo[...].T
     both = turned[:96].astype(BF16)
@@ -147,33 +231,36 @@
         ).astype(BF16)
         return carry
 
-    lax.fori_loop(0, 6, project, 0)
+    lax.fori_loop(0, 6, project, 0, unroll=2)
 
     row, col = iota((BLOCK, BLOCK), 0), iota((BLOCK, BLOCK), 1)
     row_step, col_step = step_of(row), step_of(col)
-    causal = (row - row_step == col - col_step) & (col_step <= row_step)
+    causal = (row - row_step == col - col_step) & (row_step <= col_step)
     logits[...] = base[...]
 
     def attend(b, carry):
         rows = pl.ds(pl.multiple_of(b * BLOCK, 32), BLOCK)
         lengths = aux[3, pl.ds(b, 1), :][:, :BLOCK].astype(jnp.int32)
-        allowed = causal & (col_step < lengths)
+        allowed = (causal & (row_step < lengths))[None]
+        scores = jnp.stack([
+            dot_nt(qkv[rows, 512 + h * 128 : 640 + h * 128], qkv[rows, h * 128 : h * 128 + 128])
+            for h in range(HEADS)
+        ])
+        scores = jnp.where(allowed, scores * HEAD_DIM ** (-0.5), -1e30)
+        peak = jnp.max(scores, axis=1, keepdims=True)
+        grown = jnp.where(allowed, jnp.exp(scores - peak), 0.0)
+        weighed = (grown * (1.0 / jnp.sum(grown, axis=1, keepdims=True))).astype(BF16)
         for h in range(HEADS):
-            at = h * HEAD_DIM
-            scores = dot_nt(qkv[rows, at : at + 128], qkv[rows, 512 + at : 640 + at])
-            scores = jnp.where(allowed, scores * HEAD_DIM ** (-0.5), -1e30)
-            peak = jnp.max(scores, axis=-1, keepdims=True)
-            grown = jnp.where(allowed, jnp.exp(scores - peak), 0.0)
-            weighed = (grown / jnp.sum(grown, axis=-1, keepdims=True)).astype(BF16)
-            probs[b * HEADS + h] = weighed
-            mixed[rows, at : at + 128] = jnp.dot(
-                weighed, qkv[rows, 1024 + at : 1152 + at], preferred_element_type=F32
+            part = weighed[h].T
+            probs[b * HEADS + h] = part
+            mixed[rows, h * 128 : h * 128 + 128] = jnp.dot(
+                part, qkv[rows, 1024 + h * 128 : 1152 + h * 128], preferred_element_type=F32
             ).astype(BF16)
         lifted = dot_nt(both, mixed[rows, :])
         logits[b, :, :BLOCK] = logits[b, :, :BLOCK] + lifted[:48] + lifted[48:]
         return carry
 
-    lax.fori_loop(0, BLOCKS, attend, 0)
+    lax.fori_loop(0, BLOCKS, attend, 0, unroll=4)
 
     action_row = iota((BLOCKS, PAD, 128), 1)
     real = action_row < ACTIONS
@@ -232,7 +319,7 @@
         grad_g[96 : 96 + PAD, :] += update[:PAD] + update[PAD:]
         return carry
 
-    lax.fori_loop(0, BLOCKS, backward, 0)
+    lax.fori_loop(0, BLOCKS, backward, 0, unroll=2)
 
     by_row, by_feature = grad_n[...].T, grad_g[...].T
     for p in range(32):
@@ -269,33 +356,53 @@
     grad_out[...] = by_out[pl.ds(pl.multiple_of(zh * 8, 8), 8), :] * scale
 
 
-def make_payload(w_query, w_key, w_value, w_out, heads):
-    return call(payload_kernel, shape((TILES, 16, 128), BF16), [VMEM] * 5, flops=2 * 10**6, moved=10**5)(
-        w_query, w_key, w_value, w_out, heads
-    )
-
-
-def make_normed(embeds, gain, heads):
+def make_payload(zh, w_query, w_key, w_value, w_out, q_turned, policy_turned, owner, slot, weight):
+    return call(
+        payload_kernel,
+        (shape((TILES + 1, 16, 128), BF16), shape((16, TILES, 16, 128), BF16), shape((8, 128))),
+        [SMEM] + [HBM] * 9,
+        [pltpu.VMEM((16, 512), BF16)] * 3
+        + [pltpu.VMEM((8, 1024), BF16)]
+        + [pltpu.VMEM((ACTIONS, 1024), BF16)] * 2
+        + [pltpu.VMEM((1, 32), jnp.int32)] * 2
+        + [pltpu.VMEM((1, 32), F32)]
+        + [pltpu.SemaphoreType.DMA((9,))],
+        flops=2 * 10**6,
+        moved=10**6,
+        limit=60,
+    )(zh, w_query, w_key, w_value, w_out, q_turned, policy_turned, owner, slot, weight)
+
+
+def make_normed(embeds, gain, q_turned, policy_turned, steps, actions, lengths):
     return call(
         norm_kernel,
-        (shape((768, 1024), BF16), shape((BLOCKS, 48, 128)), shape((128, 1024))),
-        [VMEM] * 3,
+        (
+            shape((768, 1024), BF16),
+            shape((BLOCKS, 48, 128)),
+            shape((128, 1024)),
+            shape((4, BLOCKS, 128)),
+        ),
+        [VMEM] * 7,
         flops=10**8,
         moved=4 * 10**6,
-    )(embeds, gain, heads)
-
-
-def make_message(zh, own, other, keep, recv):
+    )(embeds, gain, q_turned, policy_turned, steps, actions, lengths)
+
+
+def make_message(other, keep):
     return call(
-        pack_kernel, shape((16, 2 * TILES, 16, 128), BF16), [SMEM] + [VMEM] * 4, moved=2 * 10**6
-    )(zh, own, other, keep, recv)
-
-
-def make_sums(core, normed, base, mine, theirs, aux, dtype):
+        pack_kernel,
+        shape((16, TILES, 16, 128), BF16),
+        [VMEM, HBM],
+        [pltpu.VMEM((8, 128), F32), pltpu.SemaphoreType.DMA],
+        moved=10**6,
+    )(other, keep)
+
+
+def make_sums(place, normed, base, blocks, aux, dtype):
     return call(
         main_kernel,
         (shape((32, 32, 128), dtype), shape((128, 512))),
-        [SMEM] + [VMEM] * 5,
+        [SMEM] + [VMEM] * 7,
         [
             pltpu.VMEM((1024, 1536), BF16),
             pltpu.VMEM((512, 128), F32),
@@ -309,8 +416,8 @@
         ],
         flops=4 * 10**9,
         moved=10**7,
-        limit=48,
-    )(core, normed, base, mine, theirs, aux)
+        limit=22,
+    )(place, normed, base, *blocks, aux)
 
 
 def make_grads(parts, value_rows, q_rows):
@@ -327,39 +434,6 @@
     return call(
         clip_kernel, (shape((16, 512)), shape((8, 1024))), [SMEM] + [VMEM] * 3, moved=2 * 10**5
     )(zh, squares, by_value, by_out)
-
-
-def padded_heads(q_head, policy_head):
-    width = ((0, 0), (0, PAD - ACTIONS))
-    return jnp.concatenate(
-        [jnp.pad(q_head, width), jnp.pad(policy_head, width), jnp.zeros((1024, 80), BF16)], axis=1
-    )
-
-
-def row_facts(replay_steps, replay_actions, replay_lengths):
-    def lanes(array, fill):
-        flat = array.astype(F32).reshape(BLOCKS, BLOCK)
-        return jnp.pad(flat, ((0, 0), (0, 128 - BLOCK)), constant_values=fill)
-
-    lengths = jnp.broadcast_to(replay_lengths[:, None], (32, STEPS))
-    return jnp.stack([
-        lanes(replay_steps[:, 0, :], 0.0),
-        lanes(replay_steps[:, 1, :], 1.0),
-        lanes(replay_actions, 0.0),
-        lanes(lengths, 0.0),
-    ])
-
-
-def slot_weights(sample_owner, sample_slot, sample_weight, zh):
-    owner = sample_owner[:, 0]
-    place = (owner >> 4) * 8 + (owner & 7)
-    half = (owner >> 3) & 1
-    hit = (place[:, None, None] == jnp.arange(32)[None, :, None]) & (
-        sample_slot[:, None, None] == jnp.arange(128)[None, None, :]
-    )
-    weights = jnp.where(hit, sample_weight[:, None, None], 0.0)
-    stays = (half == zh)[:, None, None]
-    return jnp.sum(jnp.where(stays, weights, 0.0), axis=0), jnp.sum(jnp.where(stays, 0.0, weights), axis=0)
 
 
 def per_device(
@@ -380,21 +454,39 @@
 ):
     zh = lax.axis_index("zh").astype(jnp.int32)
     core = lax.axis_index("c").astype(jnp.int32)
-    heads = padded_heads(q_head, policy_head)
-    own = make_payload(w_query, w_key, w_value, w_out, heads)
-    other = lax.ppermute(own, ("g", "zh"), FOUR_AWAY)
-    keep, send = slot_weights(sample_owner, sample_slot, sample_weight, zh)
-    recv = lax.ppermute(send, "zh", SWAP)
-    normed, base, q_rows = make_normed(
-        replay_embed.reshape(768, 1024), norm_gain.reshape(1, 1024), heads
-    )
-    aux = row_facts(replay_steps, replay_actions, replay_lengths)
-    message = make_message(zh.reshape(1), own, other, keep, recv)
-    mine = lax.all_to_all(message, ("x", "y"), split_axis=0, concat_axis=0, tiled=True)
-    theirs = lax.ppermute(mine, "c", SWAP)
-    sums, value_rows = make_sums(core.reshape(1), normed, base, mine, theirs, aux, F32)
+    place = jnp.stack([zh, core])
+    q_turned, policy_turned = q_head.T, policy_head.T
+    own, copies, keep = make_payload(
+        zh.reshape(1),
+        w_query,
+        w_key,
+        w_value,
+        w_out,
+        q_turned,
+        policy_turned,
+        sample_owner.reshape(1, 32),
+        sample_slot.reshape(1, 32),
+        sample_weight.reshape(1, 32),
+    )
+    other = lax.ppermute(own, "zh", SWAP)
+    mine_first = lax.all_to_all(copies, ("x", "y"), split_axis=0, concat_axis=0, tiled=True)
+    normed, base, q_rows, aux = make_normed(
+        replay_embed.reshape(768, 1024),
+        norm_gain.reshape(1, 1024),
+        q_turned,
+        policy_turned,
+        replay_steps.transpose(1, 2, 0),
+        replay_actions.T,
+        replay_lengths.reshape(1, 32),
+    )
+    message = make_message(other, keep)
+    mine_last = lax.all_to_all(message, ("x", "y"), split_axis=0, concat_axis=0, tiled=True)
+    theirs_first = lax.ppermute(mine_first, "c", SWAP)
+    theirs_last = lax.ppermute(mine_last, "c", SWAP)
+    blocks = (mine_first, theirs_first, mine_last, theirs_last)
+    sums, value_rows = make_sums(place, normed, base, blocks, aux, BF16)
     parts = lax.all_to_all(sums, ("x", "y", "c"), split_axis=0, concat_axis=0, tiled=True)
-    plane = jnp.sum(parts.astype(F32), axis=0)
+    plane = jnp.sum(parts.astype(F32), axis=0).astype(BF16)
     copies = jnp.broadcast_to(plane[None], (16, 32, 128))
     planes = lax.all_to_all(copies, ("zh", "g"), split_axis=0, concat_axis=0, tiled=True)
     by_value, by_out, squares = make_grads(planes, value_rows, q_rows)

time: 154 us -> 121 us (0.79)
  blocking collectives: 79.6 us -> 51.4 us
  starting transfers between devices: 23.4 us -> 41.9 us
  local copies, waits for them, and re-layouts: 14.2 us -> 0.88 us
  Pallas kernels: 24.7 us -> 17.9 us
    all_to_all x1 -> x0, blocking collectives: 28.4 us -> none  [per_device(): lax.all_to_all(message, ('x', 'y'), split_axis=0, concat_axis=0, tiled=True)]
    all_to_all x0 -> x2, starting transfers between devices: none -> 14.3 us  [the longest x1 7.73 us: per_device(): lax.all_to_all(copies, ('x', 'y'), split_axis=0, concat_axis=0, tiled=True)]
    pallas_call x1, Pallas kernels: 21.9 us -> 12.3 us  [make_sums(): call(main_kernel, (shape((32, 32, 128), dtype), shape((128, 512))), [SMEM...]
    ppermute x3, waiting for transfers between devices: 8.44 us -> 1.9 us  [the longest x1 1.7 us: per_device(): other = lax.ppermute(own, 'zh', SWAP)]
    all_to_all x0 -> x2, waiting for transfers between devices: none -> 5.78 us  [the longest x1 5.78 us: per_device(): lax.all_to_all(message, ('x', 'y'), split_axis=0, concat_axis=0, tiled=True)]
    unnamed x34 -> x22, local copies, waits for them, and re-layouts: 5.7 us -> 0.84 us
    ppermute x3, starting transfers between devices: 23.4 us -> 27.6 us  [the longest x1 15.6 us: per_device(): other = lax.ppermute(own, 'zh', SWAP)]
    all_to_all x1, blocking collectives: 20.8 us -> 24.8 us  [per_device(): lax.all_to_all(copies, ('zh', 'g'), split_axis=0, concat_axis=0, tiled=True)]
  transfers between devices with their start and end apart: 3 -> 5, of which waited for: 1 -> 3; matrix products, arithmetic and copies ran while one was open for 6% -> 0% of each run, Pallas kernels for 1% -> 2%
where the time goes in v2:
time: 121 us
  blocking collectives  51.4 us (42%)
  starting transfers between devices  41.9 us (35%)
  Pallas kernels  17.9 us (15%)
  waiting for transfers between devices  7.68 us (6%)
    all_to_all x1, blocking collectives, per_device(): lax.all_to_all(copies, ('zh', 'g'), split_axis=0, concat_axis=0, tiled=True)  24.8 us
    ppermute x1, starting transfers between devices, per_device(): other = lax.ppermute(own, 'zh', SWAP)  15.6 us
    all_to_all x1, blocking collectives, per_device(): lax.all_to_all(jnp.broadcast_to(squares[None], (32, 8, 128)), ('x', 'y',...  13.9 us
    all_to_all x1, blocking collectives, per_device(): lax.all_to_all(sums, ('x', 'y', 'c'), split_axis=0, concat_axis=0, tiled=...  12.8 us
    pallas_call x1, Pallas kernels, make_sums(): call(main_kernel, (shape((32, 32, 128), dtype), shape((128, 512))), [SMEM...  12.3 us
    all_to_all x1, starting transfers between devices, per_device(): lax.all_to_all(copies, ('x', 'y'), split_axis=0, concat_axis=0, tiled=True)  7.73 us
    ppermute x1, starting transfers between devices, per_device(): theirs_last = lax.ppermute(mine_last, 'c', SWAP)  6.88 us
    all_to_all x1, starting transfers between devices, per_device(): lax.all_to_all(message, ('x', 'y'), split_axis=0, concat_axis=0, tiled=True)  6.58 us
  transfers between devices with their start and end apart: 5, of which 3 were waited for; matrix products, arithmetic and copies ran while one was open for 0% of the time, Pallas kernels for 2%

profile of v2, /device:TPU:1, one launch (start us, length us, event | category | flops | bytes accessed | tf_op | source)
XLA Modules:
  0.0 120.8 jit_solution(7568313126447957907)
XLA Ops:
  0.6 2.1 %shard_map.150 = (bf16[14,16,128]{2,1,0:T(8,128)(2,1)}, bf16[16,13,16,128]{3,2,1,0:T(8,128)(2,1)}, f32[8,128]{1,0:T(8,128)}) custom-call(s32[1]{0:T(128)} %bitcast.zh_ref, bf16[16,512]{1,0:T(8,128)(2,1)} %w_query_at.1, bf16[16,512]{1,0:T(8,128)(2,1)} %w_key_at.1, bf16[16,512]{1,0:T(8,128)(2,1)} %w_value_at.1, bf16[8,1024]{1,0:T(8,128)(2,1)} %w_out_at.1, ...), custom_call_target="tpu_custom_call" | custom-call | flops 2000000 | bytes 1000000 | tf_op jit(solution)/shard_map/pallas_call | solution.py:360
  2.8 0.0 copy-start.10
  2.8 0.0 copy-start.8
  2.8 7.7 %all-to-all-start = ((bf16[16,13,16,128]{3,2,1,0:T(8,128)(2,1)}), bf16[16,13,16,128]{3,2,1,0:T(8,128)(2,1)S(1)}, u32[]{:S(2)}, u32[]{:S(2)}) async-start(bf16[16,13,16,128]{3,2,1,0:T(8,128)(2,1)} %get-tuple-element.16), calls=%async_computation | async-start | bytes 1703936 | tf_op jit(solution)/shard_map/all_to_all | solution.py:472
  10.5 0.0 copy-start
  10.5 0.0 copy-start.3
  10.6 0.0 copy-start.4
  10.6 0.0 copy-start.5
  10.6 0.0 copy-start.6
  10.6 0.0 copy-start.7
  10.6 0.0 copy-start.9
  10.6 0.0 copy-done.10
  10.6 15.6 %collective-permute-start.1 = (bf16[14,16,128]{2,1,0:T(8,128)(2,1)S(1)}, bf16[14,16,128]{2,1,0:T(8,128)(2,1)S(1)}, u32[]{:S(2)}, u32[]{:S(2)}) collective-permute-start(bf16[14,16,128]{2,1,0:T(8,128)(2,1)S(1)} %copy-done.10), channel_id=1, source_target_pairs={{0,8},{8,0},{1,9},{9,1},{2,10},{10,2},{3,11},{11,3},{4,12},{12,4},... | collective-permute-start | bytes 172040 | tf_op jit(solution)/shard_map/ppermute | solution.py:471
  26.2 1.7 %collective-permute-done.1.other = bf16[14,16,128]{2,1,0:T(8,128)(2,1)S(1)} collective-permute-done((bf16[14,16,128]{2,1,0:T(8,128)(2,1)S(1)}, bf16[14,16,128]{2,1,0:T(8,128)(2,1)S(1)}, u32[]{:S(2)}, u32[]{:S(2)}) %collective-permute-start.1) | collective-permute-done | bytes 57376 | tf_op jit(solution)/shard_map/ppermute | solution.py:471
  27.9 0.0 copy-done.8
  27.9 1.2 shard_map.151
  29.1 0.0 all-to-all-done.mine_first
  29.1 6.6 %all-to-all-start.1 = ((bf16[16,13,16,128]{3,2,1,0:T(8,128)(2,1)}), bf16[16,13,16,128]{3,2,1,0:T(8,128)(2,1)S(1)}, u32[]{:S(2)}, u32[]{:S(2)}) async-start(bf16[16,13,16,128]{3,2,1,0:T(8,128)(2,1)} %shard_map.151), calls=%async_computation.1 | async-start | bytes 1703936 | tf_op jit(solution)/shard_map/all_to_all | solution.py:483
  35.7 5.2 %collective-permute-start = (bf16[16,13,16,128]{3,2,1,0:T(8,128)(2,1)S(1)}, bf16[16,13,16,128]{3,2,1,0:T(8,128)(2,1)}, u32[]{:S(2)}, u32[]{:S(2)}) collective-permute-start(bf16[16,13,16,128]{3,2,1,0:T(8,128)(2,1)S(1)} %all-to-all-done.mine_first), channel_id=1, source_target_pairs={{0,1},{1,0},{2,3},{3,2},{4,5},{5,4},{6,7},{7,6},{8,9},{9,8},{10,11... | collective-permute-start | bytes 2555912 | tf_op jit(solution)/shard_map/ppermute | solution.py:484
  40.9 5.8 %all-to-all-done.1.mine_last = bf16[16,13,16,128]{3,2,1,0:T(8,128)(2,1)S(1)} async-done(((bf16[16,13,16,128]{3,2,1,0:T(8,128)(2,1)}), bf16[16,13,16,128]{3,2,1,0:T(8,128)(2,1)S(1)}, u32[]{:S(2)}, u32[]{:S(2)}) %all-to-all-start.1) | async-done | bytes 852000 | tf_op jit(solution)/shard_map/all_to_all | solution.py:483
  46.6 6.9 %collective-permute-start.2 = (bf16[16,13,16,128]{3,2,1,0:T(8,128)(2,1)S(1)}, bf16[16,13,16,128]{3,2,1,0:T(8,128)(2,1)}, u32[]{:S(2)}, u32[]{:S(2)}) collective-permute-start(bf16[16,13,16,128]{3,2,1,0:T(8,128)(2,1)S(1)} %all-to-all-done.1.mine_last), channel_id=1, source_target_pairs={{0,1},{1,0},{2,3},{3,2},{4,5},{5,4},{6,7},{7,6},{8,9},{9,8},{10,11... | collective-permute-start | bytes 2555912 | tf_op jit(solution)/shard_map/ppermute | solution.py:485
  53.5 0.0 copy-done
  53.5 0.0 copy-done.3
  53.6 0.0 copy-done.4
  53.6 0.0 copy-done.5
  53.6 0.0 copy-done.6
  53.6 0.0 copy-done.7
  53.6 0.0 copy-done.9
  53.6 1.0 shard_map.149
  54.6 0.0 copy-start.1
  54.6 0.8 copy-done.1
  55.4 0.1 pad_add_fusion.place
  55.4 0.0 collective-permute-done.theirs_first
  55.4 0.2 collective-permute-done.2.theirs_last
  55.6 0.0 copy-start.2
  55.6 12.3 %shard_map.152 = (bf16[32,32,128]{2,1,0:T(8,128)(2,1)S(1)}, f32[128,512]{1,0:T(8,128)S(1)}) custom-call(s32[2]{0:T(128)S(1)} %pad_add_fusion.place, bf16[768,1024]{1,0:T(8,128)(2,1)S(1)} %get-tuple-element.14.normed, f32[8,48,128]{2,1,0:T(8,128)S(1)} %get-tuple-element.15.base, bf16[16,13,16,128]{3,2,1,0:T(8,128)(2,1)S(1)} %all-to-all-done.mine_first, ...), custom_call_target="tpu_custom_call" | custom-call | flops 4000000000 | bytes 10000000 | tf_op jit(solution)/shard_map/pallas_call | solution.py:402
  68.0 12.8 %all_to_all.25 = bf16[32,32,128]{2,1,0:T(8,128)(2,1)S(1)} all-to-all(bf16[32,32,128]{2,1,0:T(8,128)(2,1)S(1)} %get-tuple-element.20), channel_id=1, replica_groups=mesh['g'=8,'x'=4,'zh'=2,'y'=4,'c'=2] {'x','y','c'}, dimensions={0} | all-to-all | bytes 524288 | tf_op jit(solution)/shard_map/all_to_all | solution.py:488
  80.8 0.1 reduce_sum.12
  80.9 24.8 %all_to_all.26.parts = bf16[16,32,128]{2,1,0:T(8,128)(2,1)S(1)} all-to-all(bf16[16,32,128]{2,1,0:T(8,128)(2,1)S(1)} %broadcast_in_dim.4), channel_id=1, replica_groups=mesh['g'=8,'x'=4,'zh'=2,'y'=4,'c'=2] {'zh','g'}, dimensions={0} | all-to-all | bytes 262144 | tf_op jit(solution)/shard_map/all_to_all | solution.py:491
  105.6 0.0 copy-done.2
  105.6 0.5 shard_map.153
  106.1 13.9 %all_to_all.27.squares = f32[32,8,128]{2,1,0:T(8,128)S(1)} all-to-all(f32[32,8,128]{2,1,0:T(8,128)S(1)} %broadcast_in_dim.5), channel_id=1, replica_groups=mesh['g'=8,'x'=4,'zh'=2,'y'=4,'c'=2] {'x','y','c'}, dimensions={0} | all-to-all | bytes 262144 | tf_op jit(solution)/shard_map/all_to_all | solution.py:493
  120.0 0.8 shard_map.154
  (2 shorter events, 0.0 us)
Async XLA Ops:
  2.8 7.8 %copy-start.10 = (bf16[14,16,128]{2,1,0:T(8,128)(2,1)S(1)}, bf16[14,16,128]{2,1,0:T(8,128)(2,1)}, u32[]{:S(2)}) copy-start(bf16[14,16,128]{2,1,0:T(8,128)(2,1)} %get-tuple-element.17) | copy-start | bytes 172036
  2.8 25.1 %copy-start.8 = (f32[8,128]{1,0:T(8,128)S(1)}, f32[8,128]{1,0:T(8,128)}, u32[]{:S(2)}) copy-start(f32[8,128]{1,0:T(8,128)} %get-tuple-element.18.keep_at) | copy-start | bytes 12292
  2.8 26.3 %all-to-all-start = ((bf16[16,13,16,128]{3,2,1,0:T(8,128)(2,1)}), bf16[16,13,16,128]{3,2,1,0:T(8,128)(2,1)S(1)}, u32[]{:S(2)}, u32[]{:S(2)}) async-start(bf16[16,13,16,128]{3,2,1,0:T(8,128)(2,1)} %get-tuple-element.16), calls=%async_computation | async-start | bytes 1703936 | tf_op jit(solution)/shard_map/all_to_all | solution.py:472
  10.5 43.0 %copy-start = (bf16[32,24,1024]{2,1,0:T(8,128)(2,1)S(1)}, bf16[32,24,1024]{2,1,0:T(8,128)(2,1)}, u32[]{:S(2)}) copy-start(bf16[32,24,1024]{2,1,0:T(8,128)(2,1)} %param.14) | copy-start | bytes 4718596
  10.5 43.0 %copy-start.3 = (bf16[1024,18]{0,1:T(8,128)(2,1)S(1)}, bf16[1024,18]{0,1:T(8,128)(2,1)}, u32[]{:S(2)}) copy-start(bf16[1024,18]{0,1:T(8,128)(2,1)} %param.26) | copy-start | bytes 110596
  10.6 43.0 %copy-start.4 = (bf16[1024,18]{0,1:T(8,128)(2,1)S(1)}, bf16[1024,18]{0,1:T(8,128)(2,1)}, u32[]{:S(2)}) copy-start(bf16[1024,18]{0,1:T(8,128)(2,1)} %param.27) | copy-start | bytes 110596
  10.6 43.0 %copy-start.5 = (bf16[32,2,24]{0,2,1:T(8,128)(2,1)S(1)}, bf16[32,2,24]{0,2,1:T(8,128)(2,1)}, u32[]{:S(2)}) copy-start(bf16[32,2,24]{0,2,1:T(8,128)(2,1)} %param.15) | copy-start | bytes 9220
  10.6 43.0 %copy-start.6 = (s32[32,24]{0,1:T(8,128)S(1)}, s32[32,24]{0,1:T(8,128)}, u32[]{:S(2)}) copy-start(s32[32,24]{0,1:T(8,128)} %param.16) | copy-start | bytes 9220
  10.6 43.0 %copy-start.7 = (f32[1024]{0:T(1024)S(1)}, f32[1024]{0:T(1024)}, u32[]{:S(2)}) copy-start(f32[1024]{0:T(1024)} %param.21) | copy-start | bytes 12292
  10.6 43.0 %copy-start.9 = (s32[32]{0:T(128)S(1)}, s32[32]{0:T(128)}, u32[]{:S(2)}) copy-start(s32[32]{0:T(128)} %param.17) | copy-start | bytes 388
  10.6 17.3 %collective-permute-start.1 = (bf16[14,16,128]{2,1,0:T(8,128)(2,1)S(1)}, bf16[14,16,128]{2,1,0:T(8,128)(2,1)S(1)}, u32[]{:S(2)}, u32[]{:S(2)}) collective-permute-start(bf16[14,16,128]{2,1,0:T(8,128)(2,1)S(1)} %copy-done.10), channel_id=1, source_target_pairs={{0,8},{8,0},{1,9},{9,1},{2,10},{10,2},{3,11},{11,3},{4,12},{12,4},... | collective-permute-start | bytes 172040 | tf_op jit(solution)/shard_map/ppermute | solution.py:471
  29.1 17.6 %all-to-all-start.1 = ((bf16[16,13,16,128]{3,2,1,0:T(8,128)(2,1)}), bf16[16,13,16,128]{3,2,1,0:T(8,128)(2,1)S(1)}, u32[]{:S(2)}, u32[]{:S(2)}) async-start(bf16[16,13,16,128]{3,2,1,0:T(8,128)(2,1)} %shard_map.151), calls=%async_computation.1 | async-start | bytes 1703936 | tf_op jit(solution)/shard_map/all_to_all | solution.py:483
  35.7 19.8 %collective-permute-start = (bf16[16,13,16,128]{3,2,1,0:T(8,128)(2,1)S(1)}, bf16[16,13,16,128]{3,2,1,0:T(8,128)(2,1)}, u32[]{:S(2)}, u32[]{:S(2)}) collective-permute-start(bf16[16,13,16,128]{3,2,1,0:T(8,128)(2,1)S(1)} %all-to-all-done.mine_first), channel_id=1, source_target_pairs={{0,1},{1,0},{2,3},{3,2},{4,5},{5,4},{6,7},{7,6},{8,9},{9,8},{10,11... | collective-permute-start | bytes 2555912 | tf_op jit(solution)/shard_map/ppermute | solution.py:484
  46.6 9.0 %collective-permute-start.2 = (bf16[16,13,16,128]{3,2,1,0:T(8,128)(2,1)S(1)}, bf16[16,13,16,128]{3,2,1,0:T(8,128)(2,1)}, u32[]{:S(2)}, u32[]{:S(2)}) collective-permute-start(bf16[16,13,16,128]{3,2,1,0:T(8,128)(2,1)S(1)} %all-to-all-done.1.mine_last), channel_id=1, source_target_pairs={{0,1},{1,0},{2,3},{3,2},{4,5},{5,4},{6,7},{7,6},{8,9},{9,8},{10,11... | collective-permute-start | bytes 2555912 | tf_op jit(solution)/shard_map/ppermute | solution.py:485
  54.6 0.8 copy-start.1
  55.6 50.0 %copy-start.2 = (f32[128,1024]{1,0:T(8,128)S(1)}, f32[128,1024]{1,0:T(8,128)}, u32[]{:S(2)}) copy-start(f32[128,1024]{1,0:T(8,128)} %copy-done.1) | copy-start | bytes 1572868

commit v3 on v2

--- a/solution.py
+++ b/solution.py
@@ -212,7 +212,7 @@
                 total = total + last
         return total
 
-    total = lax.fori_loop(0, 16, unpack, jnp.zeros((16, 128), F32), unroll=2)
+    total = lax.fori_loop(0, 16, unpack, jnp.zeros((16, 128), F32), unroll=8)
     weights = total[8:9] + total[9:10]
     weights = jnp.where(c == 0, weights, pltpu.roll(weights, 96, 1))
 
@@ -231,7 +231,7 @@
         ).astype(BF16)
         return carry
 
-    lax.fori_loop(0, 6, project, 0, unroll=2)
+    lax.fori_loop(0, 6, project, 0, unroll=6)
 
     row, col = iota((BLOCK, BLOCK), 0), iota((BLOCK, BLOCK), 1)
     row_step, col_step = step_of(row), step_of(col)
@@ -256,11 +256,14 @@
             mixed[rows, h * 128 : h * 128 + 128] = jnp.dot(
                 part, qkv[rows, 1024 + h * 128 : 1152 + h * 128], preferred_element_type=F32
             ).astype(BF16)
-        lifted = dot_nt(both, mixed[rows, :])
-        logits[b, :, :BLOCK] = logits[b, :, :BLOCK] + lifted[:48] + lifted[48:]
         return carry
 
-    lax.fori_loop(0, BLOCKS, attend, 0, unroll=4)
+    lax.fori_loop(0, BLOCKS, attend, 0, unroll=8)
+
+    lifted = dot_nt(both, mixed[...])
+    lifted = lifted[:48] + lifted[48:]
+    for b in range(BLOCKS):
+        logits[b, :, :BLOCK] = logits[b, :, :BLOCK] + lifted[:, b * BLOCK : (b + 1) * BLOCK]
 
     action_row = iota((BLOCKS, PAD, 128), 1)
     real = action_row < ACTIONS
@@ -305,7 +308,7 @@
     grad_g[...] = jnp.zeros_like(grad_g)
 
     def backward(b, carry):
-        rows = pl.ds(pl.multiple_of(b * BLOCK, 32), BLOCK)
+        rows = pl.ds(b * BLOCK, BLOCK)
         given = dq[b][:, :BLOCK]
         parts = []
         for h in range(HEADS):
@@ -313,13 +316,16 @@
             parts.append(both_parts[:PAD] + both_parts[PAD:])
         high, low = split(jnp.concatenate(parts, axis=0))
         stacked = jnp.concatenate([high, low], axis=0).astype(BF16)
-        update = jnp.dot(stacked, normed[rows, :], preferred_element_type=F32)
-        grad_n[:96, :] += update[:96] + update[96:]
+        stacks.append(stacked)
         update = jnp.dot(given, mixed[rows, :], preferred_element_type=F32)
         grad_g[96 : 96 + PAD, :] += update[:PAD] + update[PAD:]
         return carry
 
-    lax.fori_loop(0, BLOCKS, backward, 0, unroll=2)
+    stacks = []
+    for b in range(BLOCKS):
+        backward(b, 0)
+    update = jnp.dot(jnp.concatenate(stacks, axis=1), normed[...], preferred_element_type=F32)
+    grad_n[:96, :] = update[:96] + update[96:]
 
     by_row, by_feature = grad_n[...].T, grad_g[...].T
     for p in range(32):

time: 121 us -> 118 us (0.975)
  Pallas kernels: 17.9 us -> 14.5 us
    pallas_call x1, Pallas kernels: 12.3 us -> 8.96 us  [make_sums(): call(main_kernel, (shape((32, 32, 128), dtype), shape((128, 512))), [SMEM...]
where the time goes in v3:
time: 118 us; the launch traced here: 117 us
  blocking collectives  51.4 us (44%)
  starting transfers between devices  41.9 us (36%)
  Pallas kernels  14.5 us (12%)
  waiting for transfers between devices  7.68 us (7%)
    all_to_all x1, blocking collectives, per_device(): lax.all_to_all(copies, ('zh', 'g'), split_axis=0, concat_axis=0, tiled=True)  24.7 us
    ppermute x1, starting transfers between devices, per_device(): other = lax.ppermute(own, 'zh', SWAP)  15.6 us
    all_to_all x1, blocking collectives, per_device(): lax.all_to_all(jnp.broadcast_to(squares[None], (32, 8, 128)), ('x', 'y',...  13.9 us
    all_to_all x1, blocking collectives, per_device(): lax.all_to_all(sums, ('x', 'y', 'c'), split_axis=0, concat_axis=0, tiled=...  12.8 us
    pallas_call x1, Pallas kernels, make_sums(): call(main_kernel, (shape((32, 32, 128), dtype), shape((128, 512))), [SMEM...  8.96 us
    all_to_all x1, starting transfers between devices, per_device(): lax.all_to_all(copies, ('x', 'y'), split_axis=0, concat_axis=0, tiled=True)  7.73 us
    ppermute x1, starting transfers between devices, per_device(): theirs_last = lax.ppermute(mine_last, 'c', SWAP)  6.88 us
    all_to_all x1, starting transfers between devices, per_device(): lax.all_to_all(message, ('x', 'y'), split_axis=0, concat_axis=0, tiled=True)  6.58 us
  transfers between devices with their start and end apart: 5, of which 3 were waited for; matrix products, arithmetic and copies ran while one was open for 0% of the time, Pallas kernels for 2%

profile of v3, /device:TPU:1, one launch (start us, length us, event | category | flops | bytes accessed | tf_op | source)
XLA Modules:
  0.0 117.4 jit_solution(12597220280236983731)
XLA Ops:
  0.6 2.1 %shard_map.150 = (bf16[14,16,128]{2,1,0:T(8,128)(2,1)}, bf16[16,13,16,128]{3,2,1,0:T(8,128)(2,1)}, f32[8,128]{1,0:T(8,128)}) custom-call(s32[1]{0:T(128)} %bitcast.zh_ref, bf16[16,512]{1,0:T(8,128)(2,1)} %w_query_at.1, bf16[16,512]{1,0:T(8,128)(2,1)} %w_key_at.1, bf16[16,512]{1,0:T(8,128)(2,1)} %w_value_at.1, bf16[8,1024]{1,0:T(8,128)(2,1)} %w_out_at.1, ...), custom_call_target="tpu_custom_call" | custom-call | flops 2000000 | bytes 1000000 | tf_op jit(solution)/shard_map/pallas_call | solution.py:366
  2.8 0.0 copy-start.10
  2.8 0.0 copy-start.8
  2.8 7.7 %all-to-all-start = ((bf16[16,13,16,128]{3,2,1,0:T(8,128)(2,1)}), bf16[16,13,16,128]{3,2,1,0:T(8,128)(2,1)S(1)}, u32[]{:S(2)}, u32[]{:S(2)}) async-start(bf16[16,13,16,128]{3,2,1,0:T(8,128)(2,1)} %get-tuple-element.16), calls=%async_computation | async-start | bytes 1703936 | tf_op jit(solution)/shard_map/all_to_all | solution.py:478
  10.5 0.0 copy-start
  10.5 0.0 copy-start.3
  10.6 0.0 copy-start.4
  10.6 0.0 copy-start.5
  10.6 0.0 copy-start.6
  10.6 0.0 copy-start.7
  10.6 0.0 copy-start.9
  10.6 0.0 copy-done.10
  10.6 15.6 %collective-permute-start.1 = (bf16[14,16,128]{2,1,0:T(8,128)(2,1)S(1)}, bf16[14,16,128]{2,1,0:T(8,128)(2,1)S(1)}, u32[]{:S(2)}, u32[]{:S(2)}) collective-permute-start(bf16[14,16,128]{2,1,0:T(8,128)(2,1)S(1)} %copy-done.10), channel_id=1, source_target_pairs={{0,8},{8,0},{1,9},{9,1},{2,10},{10,2},{3,11},{11,3},{4,12},{12,4},... | collective-permute-start | bytes 172040 | tf_op jit(solution)/shard_map/ppermute | solution.py:477
  26.2 1.7 %collective-permute-done.1.other = bf16[14,16,128]{2,1,0:T(8,128)(2,1)S(1)} collective-permute-done((bf16[14,16,128]{2,1,0:T(8,128)(2,1)S(1)}, bf16[14,16,128]{2,1,0:T(8,128)(2,1)S(1)}, u32[]{:S(2)}, u32[]{:S(2)}) %collective-permute-start.1) | collective-permute-done | bytes 57376 | tf_op jit(solution)/shard_map/ppermute | solution.py:477
  27.9 0.0 copy-done.8
  27.9 1.2 shard_map.151
  29.1 0.0 all-to-all-done.mine_first
  29.1 6.6 %all-to-all-start.1 = ((bf16[16,13,16,128]{3,2,1,0:T(8,128)(2,1)}), bf16[16,13,16,128]{3,2,1,0:T(8,128)(2,1)S(1)}, u32[]{:S(2)}, u32[]{:S(2)}) async-start(bf16[16,13,16,128]{3,2,1,0:T(8,128)(2,1)} %shard_map.151), calls=%async_computation.1 | async-start | bytes 1703936 | tf_op jit(solution)/shard_map/all_to_all | solution.py:489
  35.7 5.2 %collective-permute-start = (bf16[16,13,16,128]{3,2,1,0:T(8,128)(2,1)S(1)}, bf16[16,13,16,128]{3,2,1,0:T(8,128)(2,1)}, u32[]{:S(2)}, u32[]{:S(2)}) collective-permute-start(bf16[16,13,16,128]{3,2,1,0:T(8,128)(2,1)S(1)} %all-to-all-done.mine_first), channel_id=1, source_target_pairs={{0,1},{1,0},{2,3},{3,2},{4,5},{5,4},{6,7},{7,6},{8,9},{9,8},{10,11... | collective-permute-start | bytes 2555912 | tf_op jit(solution)/shard_map/ppermute | solution.py:490
  40.9 5.8 %all-to-all-done.1.mine_last = bf16[16,13,16,128]{3,2,1,0:T(8,128)(2,1)S(1)} async-done(((bf16[16,13,16,128]{3,2,1,0:T(8,128)(2,1)}), bf16[16,13,16,128]{3,2,1,0:T(8,128)(2,1)S(1)}, u32[]{:S(2)}, u32[]{:S(2)}) %all-to-all-start.1) | async-done | bytes 852000 | tf_op jit(solution)/shard_map/all_to_all | solution.py:489
  46.6 6.9 %collective-permute-start.2 = (bf16[16,13,16,128]{3,2,1,0:T(8,128)(2,1)S(1)}, bf16[16,13,16,128]{3,2,1,0:T(8,128)(2,1)}, u32[]{:S(2)}, u32[]{:S(2)}) collective-permute-start(bf16[16,13,16,128]{3,2,1,0:T(8,128)(2,1)S(1)} %all-to-all-done.1.mine_last), channel_id=1, source_target_pairs={{0,1},{1,0},{2,3},{3,2},{4,5},{5,4},{6,7},{7,6},{8,9},{9,8},{10,11... | collective-permute-start | bytes 2555912 | tf_op jit(solution)/shard_map/ppermute | solution.py:491
  53.5 0.0 copy-done
  53.5 0.0 copy-done.3
  53.6 0.0 copy-done.4
  53.6 0.0 copy-done.5
  53.6 0.0 copy-done.6
  53.6 0.0 copy-done.7
  53.6 0.0 copy-done.9
  53.6 1.0 shard_map.149
  54.6 0.0 copy-start.1
  54.6 0.8 copy-done.1
  55.4 0.1 pad_add_fusion.place
  55.4 0.0 collective-permute-done.theirs_first
  55.4 0.2 collective-permute-done.2.theirs_last
  55.6 0.0 copy-start.2
  55.6 9.0 %shard_map.152 = (bf16[32,32,128]{2,1,0:T(8,128)(2,1)S(1)}, f32[128,512]{1,0:T(8,128)S(1)}) custom-call(s32[2]{0:T(128)S(1)} %pad_add_fusion.place, bf16[768,1024]{1,0:T(8,128)(2,1)S(1)} %get-tuple-element.14.normed, f32[8,48,128]{2,1,0:T(8,128)S(1)} %get-tuple-element.15.base, bf16[16,13,16,128]{3,2,1,0:T(8,128)(2,1)S(1)} %all-to-all-done.mine_first, ...), custom_call_target="tpu_custom_call" | custom-call | flops 4000000000 | bytes 10000000 | tf_op jit(solution)/shard_map/pallas_call | solution.py:408
  64.6 12.8 %all_to_all.25 = bf16[32,32,128]{2,1,0:T(8,128)(2,1)S(1)} all-to-all(bf16[32,32,128]{2,1,0:T(8,128)(2,1)S(1)} %get-tuple-element.20), channel_id=1, replica_groups=mesh['g'=8,'x'=4,'zh'=2,'y'=4,'c'=2] {'x','y','c'}, dimensions={0} | all-to-all | bytes 524288 | tf_op jit(solution)/shard_map/all_to_all | solution.py:494
  77.4 0.1 reduce_sum.12
  77.5 24.7 %all_to_all.26.parts = bf16[16,32,128]{2,1,0:T(8,128)(2,1)S(1)} all-to-all(bf16[16,32,128]{2,1,0:T(8,128)(2,1)S(1)} %broadcast_in_dim.4), channel_id=1, replica_groups=mesh['g'=8,'x'=4,'zh'=2,'y'=4,'c'=2] {'zh','g'}, dimensions={0} | all-to-all | bytes 262144 | tf_op jit(solution)/shard_map/all_to_all | solution.py:497
  102.2 0.0 copy-done.2
  102.2 0.5 shard_map.153
  102.8 13.9 %all_to_all.27.squares = f32[32,8,128]{2,1,0:T(8,128)S(1)} all-to-all(f32[32,8,128]{2,1,0:T(8,128)S(1)} %broadcast_in_dim.5), channel_id=1, replica_groups=mesh['g'=8,'x'=4,'zh'=2,'y'=4,'c'=2] {'x','y','c'}, dimensions={0} | all-to-all | bytes 262144 | tf_op jit(solution)/shard_map/all_to_all | solution.py:499
  116.6 0.8 shard_map.154
  (2 shorter events, 0.0 us)
Async XLA Ops:
  2.8 7.8 %copy-start.10 = (bf16[14,16,128]{2,1,0:T(8,128)(2,1)S(1)}, bf16[14,16,128]{2,1,0:T(8,128)(2,1)}, u32[]{:S(2)}) copy-start(bf16[14,16,128]{2,1,0:T(8,128)(2,1)} %get-tuple-element.17) | copy-start | bytes 172036
  2.8 25.1 %copy-start.8 = (f32[8,128]{1,0:T(8,128)S(1)}, f32[8,128]{1,0:T(8,128)}, u32[]{:S(2)}) copy-start(f32[8,128]{1,0:T(8,128)} %get-tuple-element.18.keep_at) | copy-start | bytes 12292
  2.8 26.3 %all-to-all-start = ((bf16[16,13,16,128]{3,2,1,0:T(8,128)(2,1)}), bf16[16,13,16,128]{3,2,1,0:T(8,128)(2,1)S(1)}, u32[]{:S(2)}, u32[]{:S(2)}) async-start(bf16[16,13,16,128]{3,2,1,0:T(8,128)(2,1)} %get-tuple-element.16), calls=%async_computation | async-start | bytes 1703936 | tf_op jit(solution)/shard_map/all_to_all | solution.py:478
  10.5 43.0 %copy-start = (bf16[32,24,1024]{2,1,0:T(8,128)(2,1)S(1)}, bf16[32,24,1024]{2,1,0:T(8,128)(2,1)}, u32[]{:S(2)}) copy-start(bf16[32,24,1024]{2,1,0:T(8,128)(2,1)} %param.14) | copy-start | bytes 4718596
  10.5 43.0 %copy-start.3 = (bf16[1024,18]{0,1:T(8,128)(2,1)S(1)}, bf16[1024,18]{0,1:T(8,128)(2,1)}, u32[]{:S(2)}) copy-start(bf16[1024,18]{0,1:T(8,128)(2,1)} %param.26) | copy-start | bytes 110596
  10.6 43.0 %copy-start.4 = (bf16[1024,18]{0,1:T(8,128)(2,1)S(1)}, bf16[1024,18]{0,1:T(8,128)(2,1)}, u32[]{:S(2)}) copy-start(bf16[1024,18]{0,1:T(8,128)(2,1)} %param.27) | copy-start | bytes 110596
  10.6 43.0 %copy-start.5 = (bf16[32,2,24]{0,2,1:T(8,128)(2,1)S(1)}, bf16[32,2,24]{0,2,1:T(8,128)(2,1)}, u32[]{:S(2)}) copy-start(bf16[32,2,24]{0,2,1:T(8,128)(2,1)} %param.15) | copy-start | bytes 9220
  10.6 43.0 %copy-start.6 = (s32[32,24]{0,1:T(8,128)S(1)}, s32[32,24]{0,1:T(8,128)}, u32[]{:S(2)}) copy-start(s32[32,24]{0,1:T(8,128)} %param.16) | copy-start | bytes 9220
  10.6 43.0 %copy-start.7 = (f32[1024]{0:T(1024)S(1)}, f32[1024]{0:T(1024)}, u32[]{:S(2)}) copy-start(f32[1024]{0:T(1024)} %param.21) | copy-start | bytes 12292
  10.6 43.0 %copy-start.9 = (s32[32]{0:T(128)S(1)}, s32[32]{0:T(128)}, u32[]{:S(2)}) copy-start(s32[32]{0:T(128)} %param.17) | copy-start | bytes 388
  10.6 17.3 %collective-permute-start.1 = (bf16[14,16,128]{2,1,0:T(8,128)(2,1)S(1)}, bf16[14,16,128]{2,1,0:T(8,128)(2,1)S(1)}, u32[]{:S(2)}, u32[]{:S(2)}) collective-permute-start(bf16[14,16,128]{2,1,0:T(8,128)(2,1)S(1)} %copy-done.10), channel_id=1, source_target_pairs={{0,8},{8,0},{1,9},{9,1},{2,10},{10,2},{3,11},{11,3},{4,12},{12,4},... | collective-permute-start | bytes 172040 | tf_op jit(solution)/shard_map/ppermute | solution.py:477
  29.1 17.6 %all-to-all-start.1 = ((bf16[16,13,16,128]{3,2,1,0:T(8,128)(2,1)}), bf16[16,13,16,128]{3,2,1,0:T(8,128)(2,1)S(1)}, u32[]{:S(2)}, u32[]{:S(2)}) async-start(bf16[16,13,16,128]{3,2,1,0:T(8,128)(2,1)} %shard_map.151), calls=%async_computation.1 | async-start | bytes 1703936 | tf_op jit(solution)/shard_map/all_to_all | solution.py:489
  35.7 19.8 %collective-permute-start = (bf16[16,13,16,128]{3,2,1,0:T(8,128)(2,1)S(1)}, bf16[16,13,16,128]{3,2,1,0:T(8,128)(2,1)}, u32[]{:S(2)}, u32[]{:S(2)}) collective-permute-start(bf16[16,13,16,128]{3,2,1,0:T(8,128)(2,1)S(1)} %all-to-all-done.mine_first), channel_id=1, source_target_pairs={{0,1},{1,0},{2,3},{3,2},{4,5},{5,4},{6,7},{7,6},{8,9},{9,8},{10,11... | collective-permute-start | bytes 2555912 | tf_op jit(solution)/shard_map/ppermute | solution.py:490
  46.6 9.0 %collective-permute-start.2 = (bf16[16,13,16,128]{3,2,1,0:T(8,128)(2,1)S(1)}, bf16[16,13,16,128]{3,2,1,0:T(8,128)(2,1)}, u32[]{:S(2)}, u32[]{:S(2)}) collective-permute-start(bf16[16,13,16,128]{3,2,1,0:T(8,128)(2,1)S(1)} %all-to-all-done.1.mine_last), channel_id=1, source_target_pairs={{0,1},{1,0},{2,3},{3,2},{4,5},{5,4},{6,7},{7,6},{8,9},{9,8},{10,11... | collective-permute-start | bytes 2555912 | tf_op jit(solution)/shard_map/ppermute | solution.py:491
  54.6 0.8 copy-start.1
  55.6 46.6 %copy-start.2 = (f32[128,1024]{1,0:T(8,128)S(1)}, f32[128,1024]{1,0:T(8,128)}, u32[]{:S(2)}) copy-start(f32[128,1024]{1,0:T(8,128)} %copy-done.1) | copy-start | bytes 1572868

commit v4 on v3

--- a/solution.py
+++ b/solution.py
@@ -351,7 +351,7 @@
         for r in range(0, array.shape[0], 8):
             for k in range(0, array.shape[1], 128):
                 sums = sums + array[r : r + 8, k : k + 128]
-    squares[...] = sums
+    squares[...] = jnp.sum(sums, axis=0, keepdims=True)
 
 
 def clip_kernel(zh_ref, squares, by_value, by_out, grad_value, grad_out):
@@ -400,6 +400,7 @@
         shape((16, TILES, 16, 128), BF16),
         [VMEM, HBM],
         [pltpu.VMEM((8, 128), F32), pltpu.SemaphoreType.DMA],
+        flops=10**12,
         moved=10**6,
     )(other, keep)
 
@@ -429,7 +430,7 @@
 def make_grads(parts, value_rows, q_rows):
     return call(
         grads_kernel,
-        (shape((32, 512)), shape((16, 1024)), shape((8, 128))),
+        (shape((32, 512)), shape((16, 1024)), shape((1, 128))),
         [VMEM] * 3,
         flops=10**7,
         moved=10**6,
@@ -497,7 +498,7 @@
     planes = lax.all_to_all(copies, ("zh", "g"), split_axis=0, concat_axis=0, tiled=True)
     by_value, by_out, squares = make_grads(planes, value_rows, q_rows)
     squares = lax.all_to_all(
-        jnp.broadcast_to(squares[None], (32, 8, 128)), ("x", "y", "c"), split_axis=0, concat_axis=0, tiled=True
+        jnp.broadcast_to(squares[None], (32, 1, 128)), ("x", "y", "c"), split_axis=0, concat_axis=0, tiled=True
     )
     return make_clipped(zh.reshape(1), squares, by_value, by_out)
 

time: 118 us -> 117 us (level)
  waiting for transfers between devices: 7.68 us -> 21.3 us
  blocking collectives: 51.4 us -> 42.7 us
  starting transfers between devices: 41.9 us -> 36.6 us
    all_to_all x1, waiting for transfers between devices: 0.01 us -> 12.1 us  [per_device(): lax.all_to_all(copies, ('x', 'y'), split_axis=0, concat_axis=0, tiled=True)]
    all_to_all x1, blocking collectives: 24.7 us -> 16.8 us  [per_device(): lax.all_to_all(copies, ('zh', 'g'), split_axis=0, concat_axis=0, tiled=True)]
    all_to_all x1, starting transfers between devices: 6.58 us -> 3.77 us  [per_device(): lax.all_to_all(message, ('x', 'y'), split_axis=0, concat_axis=0, tiled=True)]
    all_to_all x1, waiting for transfers between devices: 5.78 us -> 8.12 us  [per_device(): lax.all_to_all(message, ('x', 'y'), split_axis=0, concat_axis=0, tiled=True)]
    ppermute x1, waiting for transfers between devices: 1.7 us -> 0.01 us  [per_device(): other = lax.ppermute(own, 'zh', SWAP)]
    ppermute x1, starting transfers between devices: 6.88 us -> 5.3 us  [per_device(): theirs_last = lax.ppermute(mine_last, 'c', SWAP)]
where the time goes in v4:
time: 117 us; the launch traced here: 116 us
  blocking collectives  42.7 us (36%)
  starting transfers between devices  36.6 us (31%)
  waiting for transfers between devices  21.3 us (18%)
  Pallas kernels  14.7 us (13%)
    all_to_all x1, blocking collectives, per_device(): lax.all_to_all(copies, ('zh', 'g'), split_axis=0, concat_axis=0, tiled=True)  16.8 us
    ppermute x1, starting transfers between devices, per_device(): other = lax.ppermute(own, 'zh', SWAP)  16.3 us
    all_to_all x1, blocking collectives, per_device(): lax.all_to_all(jnp.broadcast_to(squares[None], (32, 1, 128)), ('x', 'y',...  13.1 us
    all_to_all x1, blocking collectives, per_device(): lax.all_to_all(sums, ('x', 'y', 'c'), split_axis=0, concat_axis=0, tiled=...  12.8 us
    all_to_all x1, waiting for transfers between devices, per_device(): lax.all_to_all(copies, ('x', 'y'), split_axis=0, concat_axis=0, tiled=True)  12.1 us
    pallas_call x1, Pallas kernels, make_sums(): call(main_kernel, (shape((32, 32, 128), dtype), shape((128, 512))), [SMEM...  9.15 us
    all_to_all x1, waiting for transfers between devices, per_device(): lax.all_to_all(message, ('x', 'y'), split_axis=0, concat_axis=0, tiled=True)  8.12 us
    all_to_all x1, starting transfers between devices, per_device(): lax.all_to_all(copies, ('x', 'y'), split_axis=0, concat_axis=0, tiled=True)  6.81 us
  transfers between devices with their start and end apart: 5, of which 3 were waited for; matrix products, arithmetic and copies ran while one was open for 0% of the time, Pallas kernels for 2%

profile of v4, /device:TPU:1, one launch (start us, length us, event | category | flops | bytes accessed | tf_op | source)
XLA Modules:
  0.0 116.3 jit_solution(15482435878615771723)
XLA Ops:
  0.6 2.2 %shard_map.150 = (bf16[14,16,128]{2,1,0:T(8,128)(2,1)}, bf16[16,13,16,128]{3,2,1,0:T(8,128)(2,1)}, f32[8,128]{1,0:T(8,128)}) custom-call(s32[1]{0:T(128)} %bitcast.zh_ref, bf16[16,512]{1,0:T(8,128)(2,1)} %w_query_at.1, bf16[16,512]{1,0:T(8,128)(2,1)} %w_key_at.1, bf16[16,512]{1,0:T(8,128)(2,1)} %w_value_at.1, bf16[8,1024]{1,0:T(8,128)(2,1)} %w_out_at.1, ...), custom_call_target="tpu_custom_call" | custom-call | flops 2000000 | bytes 1000000 | tf_op jit(solution)/shard_map/pallas_call | solution.py:366
  2.8 0.0 copy-start.7
  2.8 16.3 %collective-permute-start.1 = (bf16[14,16,128]{2,1,0:T(8,128)(2,1)}, bf16[14,16,128]{2,1,0:T(8,128)(2,1)S(1)}, u32[]{:S(2)}, u32[]{:S(2)}) collective-permute-start(bf16[14,16,128]{2,1,0:T(8,128)(2,1)} %get-tuple-element.17), channel_id=1, source_target_pairs={{0,8},{8,0},{1,9},{9,1},{2,10},{10,2},{3,11},{11,3},{4,12},{12,4},... | collective-permute-start | bytes 172040 | tf_op jit(solution)/shard_map/ppermute | solution.py:478
  19.1 6.8 %all-to-all-start = ((bf16[16,13,16,128]{3,2,1,0:T(8,128)(2,1)}), bf16[16,13,16,128]{3,2,1,0:T(8,128)(2,1)}, u32[]{:S(2)}, u32[]{:S(2)}) async-start(bf16[16,13,16,128]{3,2,1,0:T(8,128)(2,1)} %get-tuple-element.16), calls=%async_computation | async-start | bytes 1703936 | tf_op jit(solution)/shard_map/all_to_all | solution.py:479
  25.9 0.0 collective-permute-done.1.other
  25.9 0.0 copy-done.7
  25.9 1.1 shard_map.151
  27.1 0.0 copy-start
  27.1 0.0 copy-start.1
  27.1 0.0 copy-start.2
  27.1 0.0 copy-start.3
  27.1 0.0 copy-start.4
  27.1 0.0 copy-start.5
  27.1 0.0 copy-start.6
  27.2 12.1 %all-to-all-done.mine_first = bf16[16,13,16,128]{3,2,1,0:T(8,128)(2,1)} async-done(((bf16[16,13,16,128]{3,2,1,0:T(8,128)(2,1)}), bf16[16,13,16,128]{3,2,1,0:T(8,128)(2,1)}, u32[]{:S(2)}, u32[]{:S(2)}) %all-to-all-start) | async-done | bytes 852000 | tf_op jit(solution)/shard_map/all_to_all | solution.py:479
  39.3 3.8 %all-to-all-start.1 = ((bf16[16,13,16,128]{3,2,1,0:T(8,128)(2,1)}), bf16[16,13,16,128]{3,2,1,0:T(8,128)(2,1)S(1)}, u32[]{:S(2)}, u32[]{:S(2)}) async-start(bf16[16,13,16,128]{3,2,1,0:T(8,128)(2,1)} %shard_map.151), calls=%async_computation.1 | async-start | bytes 1703936 | tf_op jit(solution)/shard_map/all_to_all | solution.py:490
  43.1 4.4 %collective-permute-start = (bf16[16,13,16,128]{3,2,1,0:T(8,128)(2,1)}, bf16[16,13,16,128]{3,2,1,0:T(8,128)(2,1)}, u32[]{:S(2)}, u32[]{:S(2)}) collective-permute-start(bf16[16,13,16,128]{3,2,1,0:T(8,128)(2,1)} %all-to-all-done.mine_first), channel_id=1, source_target_pairs={{0,1},{1,0},{2,3},{3,2},{4,5},{5,4},{6,7},{7,6},{8,9},{9,8},{10,11... | collective-permute-start | bytes 2555912 | tf_op jit(solution)/shard_map/ppermute | solution.py:491
  47.5 8.1 %all-to-all-done.1.mine_last = bf16[16,13,16,128]{3,2,1,0:T(8,128)(2,1)S(1)} async-done(((bf16[16,13,16,128]{3,2,1,0:T(8,128)(2,1)}), bf16[16,13,16,128]{3,2,1,0:T(8,128)(2,1)S(1)}, u32[]{:S(2)}, u32[]{:S(2)}) %all-to-all-start.1) | async-done | bytes 852000 | tf_op jit(solution)/shard_map/all_to_all | solution.py:490
  55.6 5.3 %collective-permute-start.2 = (bf16[16,13,16,128]{3,2,1,0:T(8,128)(2,1)S(1)}, bf16[16,13,16,128]{3,2,1,0:T(8,128)(2,1)}, u32[]{:S(2)}, u32[]{:S(2)}) collective-permute-start(bf16[16,13,16,128]{3,2,1,0:T(8,128)(2,1)S(1)} %all-to-all-done.1.mine_last), channel_id=1, source_target_pairs={{0,1},{1,0},{2,3},{3,2},{4,5},{5,4},{6,7},{7,6},{8,9},{9,8},{10,11... | collective-permute-start | bytes 2555912 | tf_op jit(solution)/shard_map/ppermute | solution.py:492
  61.0 0.0 copy-done
  61.0 0.0 copy-done.1
  61.0 0.0 copy-done.2
  61.0 0.0 copy-done.3
  61.0 0.0 copy-done.4
  61.0 0.0 copy-done.5
  61.0 0.0 copy-done.6
  61.0 1.0 shard_map.149
  62.0 0.1 pad_add_fusion.place
  62.1 0.0 collective-permute-done.theirs_first
  62.1 1.0 collective-permute-done.2.theirs_last
  63.1 9.2 %shard_map.152 = (bf16[32,32,128]{2,1,0:T(8,128)(2,1)S(1)}, f32[128,512]{1,0:T(8,128)S(1)}) custom-call(s32[2]{0:T(128)S(1)} %pad_add_fusion.place, bf16[768,1024]{1,0:T(8,128)(2,1)S(1)} %get-tuple-element.14.normed, f32[8,48,128]{2,1,0:T(8,128)S(1)} %get-tuple-element.15.base, bf16[16,13,16,128]{3,2,1,0:T(8,128)(2,1)} %all-to-all-done.mine_first, ...), custom_call_target="tpu_custom_call" | custom-call | flops 4000000000 | bytes 10000000 | tf_op jit(solution)/shard_map/pallas_call | solution.py:409
  72.2 12.8 %all_to_all.25 = bf16[32,32,128]{2,1,0:T(8,128)(2,1)S(1)} all-to-all(bf16[32,32,128]{2,1,0:T(8,128)(2,1)S(1)} %get-tuple-element.20), channel_id=1, replica_groups=mesh['g'=8,'x'=4,'zh'=2,'y'=4,'c'=2] {'x','y','c'}, dimensions={0} | all-to-all | bytes 524288 | tf_op jit(solution)/shard_map/all_to_all | solution.py:495
  85.0 0.1 reduce_sum.12
  85.1 16.8 %all_to_all.26.parts = bf16[16,32,128]{2,1,0:T(8,128)(2,1)S(1)} all-to-all(bf16[16,32,128]{2,1,0:T(8,128)(2,1)S(1)} %broadcast_in_dim.6), channel_id=1, replica_groups=mesh['g'=8,'x'=4,'zh'=2,'y'=4,'c'=2] {'zh','g'}, dimensions={0} | all-to-all | bytes 262144 | tf_op jit(solution)/shard_map/all_to_all | solution.py:498
  101.9 0.5 shard_map.153
  102.4 13.1 %all_to_all.27.squares = f32[32,1,128]{2,1,0:T(1,128)S(1)} all-to-all(f32[32,1,128]{2,1,0:T(1,128)S(1)} %broadcast_in_dim.16), channel_id=1, replica_groups=mesh['g'=8,'x'=4,'zh'=2,'y'=4,'c'=2] {'x','y','c'}, dimensions={0} | all-to-all | bytes 32768 | tf_op jit(solution)/shard_map/all_to_all | solution.py:500
  115.5 0.8 shard_map.154
  (2 shorter events, 0.0 us)
Async XLA Ops:
  2.8 23.1 %copy-start.7 = (f32[8,128]{1,0:T(8,128)S(1)}, f32[8,128]{1,0:T(8,128)}, u32[]{:S(2)}) copy-start(f32[8,128]{1,0:T(8,128)} %get-tuple-element.18.keep_at) | copy-start | bytes 12292
  2.8 23.1 %collective-permute-start.1 = (bf16[14,16,128]{2,1,0:T(8,128)(2,1)}, bf16[14,16,128]{2,1,0:T(8,128)(2,1)S(1)}, u32[]{:S(2)}, u32[]{:S(2)}) collective-permute-start(bf16[14,16,128]{2,1,0:T(8,128)(2,1)} %get-tuple-element.17), channel_id=1, source_target_pairs={{0,8},{8,0},{1,9},{9,1},{2,10},{10,2},{3,11},{11,3},{4,12},{12,4},... | collective-permute-start | bytes 172040 | tf_op jit(solution)/shard_map/ppermute | solution.py:478
  19.1 20.2 %all-to-all-start = ((bf16[16,13,16,128]{3,2,1,0:T(8,128)(2,1)}), bf16[16,13,16,128]{3,2,1,0:T(8,128)(2,1)}, u32[]{:S(2)}, u32[]{:S(2)}) async-start(bf16[16,13,16,128]{3,2,1,0:T(8,128)(2,1)} %get-tuple-element.16), calls=%async_computation | async-start | bytes 1703936 | tf_op jit(solution)/shard_map/all_to_all | solution.py:479
  27.1 33.9 %copy-start = (bf16[32,24,1024]{2,1,0:T(8,128)(2,1)S(1)}, bf16[32,24,1024]{2,1,0:T(8,128)(2,1)}, u32[]{:S(2)}) copy-start(bf16[32,24,1024]{2,1,0:T(8,128)(2,1)} %param.14) | copy-start | bytes 4718596
  27.1 33.9 %copy-start.1 = (bf16[1024,18]{0,1:T(8,128)(2,1)S(1)}, bf16[1024,18]{0,1:T(8,128)(2,1)}, u32[]{:S(2)}) copy-start(bf16[1024,18]{0,1:T(8,128)(2,1)} %param.26) | copy-start | bytes 110596
  27.1 33.9 %copy-start.2 = (bf16[1024,18]{0,1:T(8,128)(2,1)S(1)}, bf16[1024,18]{0,1:T(8,128)(2,1)}, u32[]{:S(2)}) copy-start(bf16[1024,18]{0,1:T(8,128)(2,1)} %param.27) | copy-start | bytes 110596
  27.1 33.9 %copy-start.3 = (bf16[32,2,24]{0,2,1:T(8,128)(2,1)S(1)}, bf16[32,2,24]{0,2,1:T(8,128)(2,1)}, u32[]{:S(2)}) copy-start(bf16[32,2,24]{0,2,1:T(8,128)(2,1)} %param.15) | copy-start | bytes 9220
  27.1 33.9 %copy-start.4 = (s32[32,24]{0,1:T(8,128)S(1)}, s32[32,24]{0,1:T(8,128)}, u32[]{:S(2)}) copy-start(s32[32,24]{0,1:T(8,128)} %param.16) | copy-start | bytes 9220
  27.1 33.9 %copy-start.5 = (f32[1024]{0:T(1024)S(1)}, f32[1024]{0:T(1024)}, u32[]{:S(2)}) copy-start(f32[1024]{0:T(1024)} %param.21) | copy-start | bytes 12292
  27.1 33.9 %copy-start.6 = (s32[32]{0:T(128)S(1)}, s32[32]{0:T(128)}, u32[]{:S(2)}) copy-start(s32[32]{0:T(128)} %param.17) | copy-start | bytes 388
  39.3 16.3 %all-to-all-start.1 = ((bf16[16,13,16,128]{3,2,1,0:T(8,128)(2,1)}), bf16[16,13,16,128]{3,2,1,0:T(8,128)(2,1)S(1)}, u32[]{:S(2)}, u32[]{:S(2)}) async-start(bf16[16,13,16,128]{3,2,1,0:T(8,128)(2,1)} %shard_map.151), calls=%async_computation.1 | async-start | bytes 1703936 | tf_op jit(solution)/shard_map/all_to_all | solution.py:490
  43.1 19.0 %collective-permute-start = (bf16[16,13,16,128]{3,2,1,0:T(8,128)(2,1)}, bf16[16,13,16,128]{3,2,1,0:T(8,128)(2,1)}, u32[]{:S(2)}, u32[]{:S(2)}) collective-permute-start(bf16[16,13,16,128]{3,2,1,0:T(8,128)(2,1)} %all-to-all-done.mine_first), channel_id=1, source_target_pairs={{0,1},{1,0},{2,3},{3,2},{4,5},{5,4},{6,7},{7,6},{8,9},{9,8},{10,11... | collective-permute-start | bytes 2555912 | tf_op jit(solution)/shard_map/ppermute | solution.py:491
  55.6 7.4 %collective-permute-start.2 = (bf16[16,13,16,128]{3,2,1,0:T(8,128)(2,1)S(1)}, bf16[16,13,16,128]{3,2,1,0:T(8,128)(2,1)}, u32[]{:S(2)}, u32[]{:S(2)}) collective-permute-start(bf16[16,13,16,128]{3,2,1,0:T(8,128)(2,1)S(1)} %all-to-all-done.1.mine_last), channel_id=1, source_target_pairs={{0,1},{1,0},{2,3},{3,2},{4,5},{5,4},{6,7},{7,6},{8,9},{9,8},{10,11... | collective-permute-start | bytes 2555912 | tf_op jit(solution)/shard_map/ppermute | solution.py:492

commit v5 on v4

--- a/solution.py
+++ b/solution.py
@@ -76,13 +76,12 @@
 
 
 def payload_kernel(
-    zh_ref, w_query_at, w_key_at, w_value_at, w_out_at, q_at, policy_at, owner_at, slot_at, weight_at,
+    zh_ref, w_query_at, w_key_at, w_value_at, w_out, q_turned, policy_turned, owner_at, slot_at, weight_at,
     own, copies, keep,
-    w_query, w_key, w_value, w_out, q_turned, policy_turned, owner, slot, weight, sems,
+    w_query, w_key, w_value, owner, slot, weight, sems,
 ):
     pairs = (
         (w_query_at, w_query), (w_key_at, w_key), (w_value_at, w_value),
-        (w_out_at, w_out), (q_at, q_turned), (policy_at, policy_turned),
         (owner_at, owner), (slot_at, slot), (weight_at, weight),
     )
     moves = [pltpu.make_async_copy(a, b, sems.at[k]) for k, (a, b) in enumerate(pairs)]
@@ -301,8 +300,9 @@
     live = (step < lengths) & (row_weight != 0.0)
     errors = jnp.where(live, row_weight * (taken - targets), 0.0)
     high, low = split(errors)
-    dq[:, :PAD, :] = jnp.where(picked, high[:, None, :], 0.0).astype(BF16)
-    dq[:, PAD:, :] = jnp.where(picked, low[:, None, :], 0.0).astype(BF16)
+    dq[...] = jnp.concatenate(
+        [jnp.where(picked, high[:, None, :], 0.0), jnp.where(picked, low[:, None, :], 0.0)], axis=1
+    ).astype(BF16)
 
     grad_n[...] = jnp.zeros_like(grad_n)
     grad_g[...] = jnp.zeros_like(grad_g)
@@ -366,13 +366,11 @@
     return call(
         payload_kernel,
         (shape((TILES + 1, 16, 128), BF16), shape((16, TILES, 16, 128), BF16), shape((8, 128))),
-        [SMEM] + [HBM] * 9,
+        [SMEM] + [HBM] * 3 + [VMEM] * 3 + [HBM] * 3,
         [pltpu.VMEM((16, 512), BF16)] * 3
-        + [pltpu.VMEM((8, 1024), BF16)]
-        + [pltpu.VMEM((ACTIONS, 1024), BF16)] * 2
         + [pltpu.VMEM((1, 32), jnp.int32)] * 2
         + [pltpu.VMEM((1, 32), F32)]
-        + [pltpu.SemaphoreType.DMA((9,))],
+        + [pltpu.SemaphoreType.DMA((6,))],
         flops=2 * 10**6,
         moved=10**6,
         limit=60,

time: 117 us -> 118 us (level)
  no operation moved by 1% of the time
where the time goes in v5:
time: 118 us; the launch traced here: 117 us
  blocking collectives  42.7 us (36%)
  starting transfers between devices  36.6 us (31%)
  waiting for transfers between devices  21.3 us (18%)
  Pallas kernels  15.4 us (13%)
    all_to_all x1, blocking collectives, per_device(): lax.all_to_all(copies, ('zh', 'g'), split_axis=0, concat_axis=0, tiled=True)  16.8 us
    ppermute x1, starting transfers between devices, per_device(): other = lax.ppermute(own, 'zh', SWAP)  16.3 us
    all_to_all x1, blocking collectives, per_device(): lax.all_to_all(jnp.broadcast_to(squares[None], (32, 1, 128)), ('x', 'y',...  13.1 us
    all_to_all x1, blocking collectives, per_device(): lax.all_to_all(sums, ('x', 'y', 'c'), split_axis=0, concat_axis=0, tiled=...  12.8 us
    all_to_all x1, waiting for transfers between devices, per_device(): lax.all_to_all(copies, ('x', 'y'), split_axis=0, concat_axis=0, tiled=True)  12.1 us
    pallas_call x1, Pallas kernels, make_sums(): call(main_kernel, (shape((32, 32, 128), dtype), shape((128, 512))), [SMEM...  9.15 us
    all_to_all x1, waiting for transfers between devices, per_device(): lax.all_to_all(message, ('x', 'y'), split_axis=0, concat_axis=0, tiled=True)  8.12 us
    all_to_all x1, starting transfers between devices, per_device(): lax.all_to_all(copies, ('x', 'y'), split_axis=0, concat_axis=0, tiled=True)  6.81 us
  transfers between devices with their start and end apart: 5, of which 3 were waited for; matrix products, arithmetic and copies ran while one was open for 0% of the time, Pallas kernels for 2%

profile of v5, /device:TPU:1, one launch (start us, length us, event | category | flops | bytes accessed | tf_op | source)
XLA Modules:
  0.0 117.0 jit_solution(11741396203167916579)
XLA Ops:
  0.6 2.8 %shard_map.150 = (bf16[14,16,128]{2,1,0:T(8,128)(2,1)}, bf16[16,13,16,128]{3,2,1,0:T(8,128)(2,1)}, f32[8,128]{1,0:T(8,128)}) custom-call(s32[1]{0:T(128)} %bitcast.zh_ref, bf16[16,512]{1,0:T(8,128)(2,1)} %w_query_at.1, bf16[16,512]{1,0:T(8,128)(2,1)} %w_key_at.1, bf16[16,512]{1,0:T(8,128)(2,1)} %w_value_at.1, bf16[8,1024]{1,0:T(8,128)(2,1)} %w_out.1, ...), custom_call_target="tpu_custom_call" | custom-call | flops 2000000 | bytes 1000000 | tf_op jit(solution)/shard_map/pallas_call | solution.py:366
  3.5 0.0 copy-start.7
  3.5 16.3 %collective-permute-start.1 = (bf16[14,16,128]{2,1,0:T(8,128)(2,1)}, bf16[14,16,128]{2,1,0:T(8,128)(2,1)S(1)}, u32[]{:S(2)}, u32[]{:S(2)}) collective-permute-start(bf16[14,16,128]{2,1,0:T(8,128)(2,1)} %get-tuple-element.17), channel_id=1, source_target_pairs={{0,8},{8,0},{1,9},{9,1},{2,10},{10,2},{3,11},{11,3},{4,12},{12,4},... | collective-permute-start | bytes 172040 | tf_op jit(solution)/shard_map/ppermute | solution.py:476
  19.8 6.8 %all-to-all-start = ((bf16[16,13,16,128]{3,2,1,0:T(8,128)(2,1)}), bf16[16,13,16,128]{3,2,1,0:T(8,128)(2,1)}, u32[]{:S(2)}, u32[]{:S(2)}) async-start(bf16[16,13,16,128]{3,2,1,0:T(8,128)(2,1)} %get-tuple-element.16), calls=%async_computation | async-start | bytes 1703936 | tf_op jit(solution)/shard_map/all_to_all | solution.py:477
  26.6 0.0 collective-permute-done.1.other
  26.6 0.0 copy-done.7
  26.6 1.1 shard_map.151
  27.7 0.0 copy-start
  27.8 0.0 copy-start.1
  27.8 0.0 copy-start.2
  27.8 0.0 copy-start.3
  27.8 0.0 copy-start.4
  27.8 0.0 copy-start.5
  27.8 0.0 copy-start.6
  27.8 12.1 %all-to-all-done.mine_first = bf16[16,13,16,128]{3,2,1,0:T(8,128)(2,1)} async-done(((bf16[16,13,16,128]{3,2,1,0:T(8,128)(2,1)}), bf16[16,13,16,128]{3,2,1,0:T(8,128)(2,1)}, u32[]{:S(2)}, u32[]{:S(2)}) %all-to-all-start) | async-done | bytes 852000 | tf_op jit(solution)/shard_map/all_to_all | solution.py:477
  40.0 3.8 %all-to-all-start.1 = ((bf16[16,13,16,128]{3,2,1,0:T(8,128)(2,1)}), bf16[16,13,16,128]{3,2,1,0:T(8,128)(2,1)S(1)}, u32[]{:S(2)}, u32[]{:S(2)}) async-start(bf16[16,13,16,128]{3,2,1,0:T(8,128)(2,1)} %shard_map.151), calls=%async_computation.1 | async-start | bytes 1703936 | tf_op jit(solution)/shard_map/all_to_all | solution.py:488
  43.8 4.4 %collective-permute-start = (bf16[16,13,16,128]{3,2,1,0:T(8,128)(2,1)}, bf16[16,13,16,128]{3,2,1,0:T(8,128)(2,1)}, u32[]{:S(2)}, u32[]{:S(2)}) collective-permute-start(bf16[16,13,16,128]{3,2,1,0:T(8,128)(2,1)} %all-to-all-done.mine_first), channel_id=1, source_target_pairs={{0,1},{1,0},{2,3},{3,2},{4,5},{5,4},{6,7},{7,6},{8,9},{9,8},{10,11... | collective-permute-start | bytes 2555912 | tf_op jit(solution)/shard_map/ppermute | solution.py:489
  48.2 8.1 %all-to-all-done.1.mine_last = bf16[16,13,16,128]{3,2,1,0:T(8,128)(2,1)S(1)} async-done(((bf16[16,13,16,128]{3,2,1,0:T(8,128)(2,1)}), bf16[16,13,16,128]{3,2,1,0:T(8,128)(2,1)S(1)}, u32[]{:S(2)}, u32[]{:S(2)}) %all-to-all-start.1) | async-done | bytes 852000 | tf_op jit(solution)/shard_map/all_to_all | solution.py:488
  56.3 5.3 %collective-permute-start.2 = (bf16[16,13,16,128]{3,2,1,0:T(8,128)(2,1)S(1)}, bf16[16,13,16,128]{3,2,1,0:T(8,128)(2,1)}, u32[]{:S(2)}, u32[]{:S(2)}) collective-permute-start(bf16[16,13,16,128]{3,2,1,0:T(8,128)(2,1)S(1)} %all-to-all-done.1.mine_last), channel_id=1, source_target_pairs={{0,1},{1,0},{2,3},{3,2},{4,5},{5,4},{6,7},{7,6},{8,9},{9,8},{10,11... | collective-permute-start | bytes 2555912 | tf_op jit(solution)/shard_map/ppermute | solution.py:490
  61.6 0.0 copy-done
  61.6 0.0 copy-done.1
  61.6 0.0 copy-done.2
  61.7 0.0 copy-done.3
  61.7 0.0 copy-done.4
  61.7 0.0 copy-done.5
  61.7 0.0 copy-done.6
  61.7 1.0 shard_map.149
  62.7 0.1 pad_add_fusion.place
  62.7 0.0 collective-permute-done.theirs_first
  62.8 1.0 collective-permute-done.2.theirs_last
  63.7 9.1 %shard_map.152 = (bf16[32,32,128]{2,1,0:T(8,128)(2,1)S(1)}, f32[128,512]{1,0:T(8,128)S(1)}) custom-call(s32[2]{0:T(128)S(1)} %pad_add_fusion.place, bf16[768,1024]{1,0:T(8,128)(2,1)S(1)} %get-tuple-element.14.normed, f32[8,48,128]{2,1,0:T(8,128)S(1)} %get-tuple-element.15.base, bf16[16,13,16,128]{3,2,1,0:T(8,128)(2,1)} %all-to-all-done.mine_first, ...), custom_call_target="tpu_custom_call" | custom-call | flops 4000000000 | bytes 10000000 | tf_op jit(solution)/shard_map/pallas_call | solution.py:407
  72.9 12.8 %all_to_all.25 = bf16[32,32,128]{2,1,0:T(8,128)(2,1)S(1)} all-to-all(bf16[32,32,128]{2,1,0:T(8,128)(2,1)S(1)} %get-tuple-element.20), channel_id=1, replica_groups=mesh['g'=8,'x'=4,'zh'=2,'y'=4,'c'=2] {'x','y','c'}, dimensions={0} | all-to-all | bytes 524288 | tf_op jit(solution)/shard_map/all_to_all | solution.py:493
  85.7 0.1 reduce_sum.12
  85.8 16.8 %all_to_all.26.parts = bf16[16,32,128]{2,1,0:T(8,128)(2,1)S(1)} all-to-all(bf16[16,32,128]{2,1,0:T(8,128)(2,1)S(1)} %broadcast_in_dim.6), channel_id=1, replica_groups=mesh['g'=8,'x'=4,'zh'=2,'y'=4,'c'=2] {'zh','g'}, dimensions={0} | all-to-all | bytes 262144 | tf_op jit(solution)/shard_map/all_to_all | solution.py:496
  102.6 0.5 shard_map.153
  103.1 13.1 %all_to_all.27.squares = f32[32,1,128]{2,1,0:T(1,128)S(1)} all-to-all(f32[32,1,128]{2,1,0:T(1,128)S(1)} %broadcast_in_dim.16), channel_id=1, replica_groups=mesh['g'=8,'x'=4,'zh'=2,'y'=4,'c'=2] {'x','y','c'}, dimensions={0} | all-to-all | bytes 32768 | tf_op jit(solution)/shard_map/all_to_all | solution.py:498
  116.2 0.8 shard_map.154
  (2 shorter events, 0.0 us)
Async XLA Ops:
  3.5 23.1 %copy-start.7 = (f32[8,128]{1,0:T(8,128)S(1)}, f32[8,128]{1,0:T(8,128)}, u32[]{:S(2)}) copy-start(f32[8,128]{1,0:T(8,128)} %get-tuple-element.18.keep_at) | copy-start | bytes 12292
  3.5 23.1 %collective-permute-start.1 = (bf16[14,16,128]{2,1,0:T(8,128)(2,1)}, bf16[14,16,128]{2,1,0:T(8,128)(2,1)S(1)}, u32[]{:S(2)}, u32[]{:S(2)}) collective-permute-start(bf16[14,16,128]{2,1,0:T(8,128)(2,1)} %get-tuple-element.17), channel_id=1, source_target_pairs={{0,8},{8,0},{1,9},{9,1},{2,10},{10,2},{3,11},{11,3},{4,12},{12,4},... | collective-permute-start | bytes 172040 | tf_op jit(solution)/shard_map/ppermute | solution.py:476
  19.8 20.2 %all-to-all-start = ((bf16[16,13,16,128]{3,2,1,0:T(8,128)(2,1)}), bf16[16,13,16,128]{3,2,1,0:T(8,128)(2,1)}, u32[]{:S(2)}, u32[]{:S(2)}) async-start(bf16[16,13,16,128]{3,2,1,0:T(8,128)(2,1)} %get-tuple-element.16), calls=%async_computation | async-start | bytes 1703936 | tf_op jit(solution)/shard_map/all_to_all | solution.py:477
  27.7 33.9 %copy-start = (bf16[32,24,1024]{2,1,0:T(8,128)(2,1)S(1)}, bf16[32,24,1024]{2,1,0:T(8,128)(2,1)}, u32[]{:S(2)}) copy-start(bf16[32,24,1024]{2,1,0:T(8,128)(2,1)} %param.14) | copy-start | bytes 4718596
  27.8 33.9 %copy-start.1 = (bf16[1024,18]{0,1:T(8,128)(2,1)S(1)}, bf16[1024,18]{0,1:T(8,128)(2,1)}, u32[]{:S(2)}) copy-start(bf16[1024,18]{0,1:T(8,128)(2,1)} %param.26) | copy-start | bytes 110596
  27.8 33.9 %copy-start.2 = (bf16[1024,18]{0,1:T(8,128)(2,1)S(1)}, bf16[1024,18]{0,1:T(8,128)(2,1)}, u32[]{:S(2)}) copy-start(bf16[1024,18]{0,1:T(8,128)(2,1)} %param.27) | copy-start | bytes 110596
  27.8 33.9 %copy-start.3 = (bf16[32,2,24]{0,2,1:T(8,128)(2,1)S(1)}, bf16[32,2,24]{0,2,1:T(8,128)(2,1)}, u32[]{:S(2)}) copy-start(bf16[32,2,24]{0,2,1:T(8,128)(2,1)} %param.15) | copy-start | bytes 9220
  27.8 33.9 %copy-start.4 = (s32[32,24]{0,1:T(8,128)S(1)}, s32[32,24]{0,1:T(8,128)}, u32[]{:S(2)}) copy-start(s32[32,24]{0,1:T(8,128)} %param.16) | copy-start | bytes 9220
  27.8 33.9 %copy-start.5 = (f32[1024]{0:T(1024)S(1)}, f32[1024]{0:T(1024)}, u32[]{:S(2)}) copy-start(f32[1024]{0:T(1024)} %param.21) | copy-start | bytes 12292
  27.8 33.9 %copy-start.6 = (s32[32]{0:T(128)S(1)}, s32[32]{0:T(128)}, u32[]{:S(2)}) copy-start(s32[32]{0:T(128)} %param.17) | copy-start | bytes 388
  40.0 16.3 %all-to-all-start.1 = ((bf16[16,13,16,128]{3,2,1,0:T(8,128)(2,1)}), bf16[16,13,16,128]{3,2,1,0:T(8,128)(2,1)S(1)}, u32[]{:S(2)}, u32[]{:S(2)}) async-start(bf16[16,13,16,128]{3,2,1,0:T(8,128)(2,1)} %shard_map.151), calls=%async_computation.1 | async-start | bytes 1703936 | tf_op jit(solution)/shard_map/all_to_all | solution.py:488
  43.8 19.0 %collective-permute-start = (bf16[16,13,16,128]{3,2,1,0:T(8,128)(2,1)}, bf16[16,13,16,128]{3,2,1,0:T(8,128)(2,1)}, u32[]{:S(2)}, u32[]{:S(2)}) collective-permute-start(bf16[16,13,16,128]{3,2,1,0:T(8,128)(2,1)} %all-to-all-done.mine_first), channel_id=1, source_target_pairs={{0,1},{1,0},{2,3},{3,2},{4,5},{5,4},{6,7},{7,6},{8,9},{9,8},{10,11... | collective-permute-start | bytes 2555912 | tf_op jit(solution)/shard_map/ppermute | solution.py:489
  56.3 7.4 %collective-permute-start.2 = (bf16[16,13,16,128]{3,2,1,0:T(8,128)(2,1)S(1)}, bf16[16,13,16,128]{3,2,1,0:T(8,128)(2,1)}, u32[]{:S(2)}, u32[]{:S(2)}) collective-permute-start(bf16[16,13,16,128]{3,2,1,0:T(8,128)(2,1)S(1)} %all-to-all-done.1.mine_last), channel_id=1, source_target_pairs={{0,1},{1,0},{2,3},{3,2},{4,5},{5,4},{6,7},{7,6},{8,9},{9,8},{10,11... | collective-permute-start | bytes 2555912 | tf_op jit(solution)/shard_map/ppermute | solution.py:490
